TPU v7x, 32 devices: a whole 2x2x4 slice. The times are simulated.
32 devices in a mesh: dom: 8 (over y, x, core), lat: 4 (over z).
Axes of the slice: x: 2, y: 2, z: 4, core: 2. Of those that a mesh axis runs over, the one named last changes fastest.
Arguments:
- states: float32 [3, 16, 64, 1024], P(None, 'dom', 'lat'), may hold values from -3 to 3
- stir_noise: float32 [2, 16, 64, 1024], P(None, 'dom', 'lat'), may hold values from -1.2 to 1.2
- ancestors: int32 [2, 8, 2], replicated, may hold values from 0 to 3, as said below
Outputs:
- filtered: float32 [3, 16, 64, 1024], P(None, 'dom', 'lat')
Inputs may be any that keep to these rules, and one draw needn't show every extreme that they name: An entry from 2 upward names a particle of the preceding island on the loop; in every row ancestors[c, i, :] exactly one entry is 2 or more.
All inputs are finite; a program needn't handle non-finite values.
Results may differ from a plain program's by a relative error of at most 0.0003.
Values sent between devices are 32-bit elements; how exact they have to be, the bound alone decides.
No kernel may reach another device: no remote copies, remote signals or barrier semaphores. Data moves between devices by JAX's collectives and lax.ppermute only.
A program may use at most 64 MiB of HBM per device.

v0:
```python
import jax
import jax.numpy as jnp
from jax import lax
from jax.sharding import PartitionSpec as P

STEPS = 2
FILTER_ROUNDS = 2


time_step = 0.2
viscosity = 0.05
rotation = 0.3


def extended(value, sides, width):
    for axis, dim in sides:
        devices, length = (lax.axis_size(axis), value.shape[dim])
        up = [(i, (i + 1) % devices) for i in range(devices - 1)]
        down = [(j, i) for i, j in up]
        last = lax.slice_in_dim(value, length - width, length, axis=dim)
        leading = lax.slice_in_dim(value, 0, width, axis=dim)
        before = lax.ppermute(last, axis, up)
        after = lax.ppermute(leading, axis, down)
        value = jnp.concatenate([before, value, after], axis=dim)
    return value


def shifted(value, axis, steps):
    count = lax.axis_size(axis)
    pairs = [(source, (source + steps) % count) for source in range(count)]
    return lax.ppermute(value, axis, pairs)


def eastward(field_amount):
    return jnp.roll(field_amount, -1, axis=-1)


def westward(field_amount):
    return jnp.roll(field_amount, 1, axis=-1)


def slope_x(field_amount):
    return (eastward(field_amount) - westward(field_amount)) * 0.5


def slope_y(field_amount):
    return (field_amount[..., 2:, :] - field_amount[..., :-2, :]) * 0.5


def laplace(field_amount, middle):
    return (
        eastward(middle)
        + westward(middle)
        + field_amount[..., 2:, :]
        + field_amount[..., :-2, :]
        - 4.0 * middle
    )


def tendency(padded, coriolis):
    height = padded[0]
    zonal = padded[1]
    northward = padded[2]
    height_mid = height[..., 1:-1, :]
    zonal_mid = zonal[..., 1:-1, :]
    north_mid = northward[..., 1:-1, :]
    column_depth = 1.0 + height
    flux_east = column_depth[..., 1:-1, :] * zonal_mid
    flux_north = column_depth * northward
    tend_height = (
        -slope_x(flux_east) - slope_y(flux_north) + viscosity * laplace(height, height_mid)
    )
    tend_zonal = (
        -zonal_mid * slope_x(zonal_mid)
        - north_mid * slope_y(zonal)
        + coriolis * north_mid
        - slope_x(height_mid)
        + viscosity * laplace(zonal, zonal_mid)
    )
    tend_north = (
        -zonal_mid * slope_x(north_mid)
        - north_mid * slope_y(northward)
        - coriolis * zonal_mid
        - slope_y(height)
        + viscosity * laplace(northward, north_mid)
    )
    return jnp.stack([tend_height, tend_zonal, tend_north])


def coriolis_rows(start_row, row_count, all_rows):
    row_index = start_row + jnp.arange(row_count, dtype=jnp.int32)
    return (rotation * (2.0 * (row_index.astype(jnp.float32) + 0.5) / all_rows - 1.0))[:, None]


def inside_rows(start_row, row_count, all_rows):
    row_index = start_row + jnp.arange(row_count, dtype=jnp.int32)
    return ((row_index >= 0) & (row_index < all_rows))[:, None]


def wide_heun(wide, margin, first_row, local_rows, total_rows):
    inner = margin - 1
    section = wide[..., 1:-1, :] + time_step * tendency(
        wide, coriolis_rows(first_row - inner, local_rows + 2 * inner, total_rows)
    )
    section = jnp.where(
        inside_rows(first_row - inner, local_rows + 2 * inner, total_rows), section, 0.0
    )
    outer = margin - 2
    updated = 0.5 * (
        wide[..., 2:-2, :]
        + section[..., 1:-1, :]
        + time_step
        * tendency(section, coriolis_rows(first_row - outer, local_rows + 2 * outer, total_rows))
    )
    return jnp.where(
        inside_rows(first_row - outer, local_rows + 2 * outer, total_rows), updated, 0.0
    )


def choose(candidates, wanted):
    result = candidates[:, 0]
    for source_slot in range(1, candidates.shape[1]):
        result = jnp.where(wanted == source_slot, candidates[:, source_slot], result)
    return result


def body(states, stir_noise, ancestors):
    per_island = states.shape[1]
    local_rows = states.shape[2]
    total_rows = local_rows * lax.axis_size("lat")
    first_row = lax.axis_index("lat") * local_rows
    island = lax.axis_index("dom")
    fields = states
    for cycle_idx in range(FILTER_ROUNDS):
        wide = extended(fields, (("lat", 2),), 2 * STEPS)
        for step_idx in range(STEPS):
            wide = wide_heun(wide, 2 * (STEPS - step_idx), first_row, local_rows, total_rows)
        fields = wide
        fields = jnp.concatenate([fields[0:1] + stir_noise[cycle_idx][None], fields[1:]], axis=0)
        cycle_parents = ancestors[cycle_idx]
        parent_row = lax.dynamic_index_in_dim(cycle_parents, island, 0, keepdims=False)
        arrived = shifted(fields, "dom", 1)
        candidates = jnp.concatenate([fields, arrived], axis=1)
        fields = jnp.stack(
            [choose(candidates, parent_row[target_slot]) for target_slot in range(per_island)],
            axis=1,
        )
    return fields


def solution(mesh):
    in_specs = (P(None, "dom", "lat", None), P(None, "dom", "lat", None), P())
    out_specs = P(None, "dom", "lat", None)
    return jax.shard_map(body, mesh=mesh, in_specs=in_specs, out_specs=out_specs, check_vma=False)
```

profile of v0, /device:TPU:0, one launch (start us, length us, event | category | flops | bytes accessed | tf_op | source)
XLA Modules:
  0.0 55.0 jit_solution(1922968696755402640)
XLA Ops:
  0.0 1.1 %fusion.92 = (f32[3,2,4,1024]{3,2,1,0:T(4,128)S(1)}, f32[3,2,4,1024]{3,2,1,0:T(4,128)S(1)}) fusion(f32[3,2,16,1024]{3,2,1,0:T(8,128)} %param.3), kind=kLoop, calls=%fused_computation.271 | loop fusion | bytes 393216 | tf_op jit(solution)/shard_map/slice | solution.py:20
  1.1 4.9 %collective-permute-start = (f32[3,2,4,1024]{3,2,1,0:T(4,128)S(1)}, f32[3,2,4,1024]{3,2,1,0:T(4,128)S(1)}, u32[]{:S(2)}, u32[]{:S(2)}) collective-permute-start(f32[3,2,4,1024]{3,2,1,0:T(4,128)S(1)} %get-tuple-element.51), channel_id=1, source_target_pairs={{0,1},{1,2},{2,3},{4,5},{5,6},{6,7},{8,9},{9,10},{10,11},{12,13},{... | collective-permute-start | bytes 294920 | tf_op jit(solution)/shard_map/ppermute | solution.py:22
  6.1 1.3 %collective-permute-start.1 = (f32[3,2,4,1024]{3,2,1,0:T(4,128)S(1)}, f32[3,2,4,1024]{3,2,1,0:T(4,128)S(1)}, u32[]{:S(2)}, u32[]{:S(2)}) collective-permute-start(f32[3,2,4,1024]{3,2,1,0:T(4,128)S(1)} %get-tuple-element.52), channel_id=1, source_target_pairs={{1,0},{2,1},{3,2},{5,4},{6,5},{7,6},{9,8},{10,9},{11,10},{13,12},{... | collective-permute-start | bytes 294920 | tf_op jit(solution)/shard_map/ppermute | solution.py:23
  7.5 0.8 %collective-permute-done = f32[3,2,4,1024]{3,2,1,0:T(4,128)S(1)} collective-permute-done((f32[3,2,4,1024]{3,2,1,0:T(4,128)S(1)}, f32[3,2,4,1024]{3,2,1,0:T(4,128)S(1)}, u32[]{:S(2)}, u32[]{:S(2)}) %collective-permute-start) | collective-permute-done | bytes 98336 | tf_op jit(solution)/shard_map/ppermute | solution.py:22
  8.2 4.3 %collective-permute-done.1 = f32[3,2,4,1024]{3,2,1,0:T(4,128)S(1)} collective-permute-done((f32[3,2,4,1024]{3,2,1,0:T(4,128)S(1)}, f32[3,2,4,1024]{3,2,1,0:T(4,128)S(1)}, u32[]{:S(2)}, u32[]{:S(2)}) %collective-permute-start.1) | collective-permute-done | bytes 98336 | tf_op jit(solution)/shard_map/ppermute | solution.py:23
  13.0 0.2 slice_multiply_fusion.11
  13.4 0.2 fusion.147
  13.7 0.3 add_bitcast_fusion.11
  13.9 0.2 fusion.53
  14.2 0.2 fusion.9
  14.6 0.2 slice_multiply_fusion.9
  15.5 0.3 add_bitcast_fusion.9
  15.7 0.2 fusion.47
  16.0 0.2 fusion.8
  16.5 0.2 slice_multiply_fusion.7
  17.3 0.3 add_bitcast_fusion.7
  17.6 0.2 fusion.41
  17.8 0.2 fusion.5
  18.3 0.2 slice_multiply_fusion.15
  19.0 0.2 add_bitcast_fusion.15
  19.2 0.1 fusion.77
  19.4 0.2 fusion.15
  19.6 0.9 %copy-done.1 = f32[2,2,16,1024]{3,2,1,0:T(8,128)S(1)} copy-done((f32[2,2,16,1024]{3,2,1,0:T(8,128)S(1)}, f32[2,2,16,1024]{3,2,1,0:T(8,128)}, u32[]{:S(2)}) %copy-start.1) | copy-done | bytes 262168
  20.6 0.6 %copy-done.2 = s32[2,8,2]{1,2,0:T(2,128)S(1)} copy-done((s32[2,8,2]{1,2,0:T(2,128)S(1)}, s32[2,8,2]{1,2,0:T(2,128)}, u32[]{:S(2)}) %copy-start.2) | copy-done | bytes 152
  21.3 0.6 %fusion.159 = (s32[1,1,1]{1,2,0:T(1,128)}, s32[1,1,1]{1,2,0:T(1,128)}) fusion(s32[1,1,2]{1,2,0:T(2,128)S(1)} %get-tuple-element.203), kind=kLoop, calls=%fused_computation.338 | loop fusion | bytes 16 | tf_op jit(solution)/shard_map/slice | solution.py:145
  25.7 3.0 %collective-permute-done.2 = f32[3,2,16,1024]{3,2,1,0:T(8,128)S(1)} collective-permute-done((f32[3,2,16,1024]{3,2,1,0:T(8,128)S(1)}, f32[3,2,16,1024]{3,2,1,0:T(8,128)S(1)}, u32[]{:S(2)}, u32[]{:S(2)}) %collective-permute-start.2) | collective-permute-done | bytes 393248 | tf_op jit(solution)/shard_map/ppermute | solution.py:31
  28.8 3.5 %collective-permute-start.3 = (f32[3,2,4,1024]{3,2,1,0:T(4,128)S(1)}, f32[3,2,4,1024]{3,2,1,0:T(4,128)S(1)}, u32[]{:S(2)}, u32[]{:S(2)}) collective-permute-start(f32[3,2,4,1024]{3,2,1,0:T(4,128)S(1)} %get-tuple-element.49), channel_id=1, source_target_pairs={{0,1},{1,2},{2,3},{4,5},{5,6},{6,7},{8,9},{9,10},{10,11},{12,13},{... | collective-permute-start | bytes 294920 | tf_op jit(solution)/shard_map/ppermute | solution.py:22
  32.3 1.3 %collective-permute-start.4 = (f32[3,2,4,1024]{3,2,1,0:T(4,128)S(1)}, f32[3,2,4,1024]{3,2,1,0:T(4,128)S(1)}, u32[]{:S(2)}, u32[]{:S(2)}) collective-permute-start(f32[3,2,4,1024]{3,2,1,0:T(4,128)S(1)} %get-tuple-element.50), channel_id=1, source_target_pairs={{1,0},{2,1},{3,2},{5,4},{6,5},{7,6},{9,8},{10,9},{11,10},{13,12},{... | collective-permute-start | bytes 294920 | tf_op jit(solution)/shard_map/ppermute | solution.py:23
  33.6 0.9 %collective-permute-done.3 = f32[3,2,4,1024]{3,2,1,0:T(4,128)S(1)} collective-permute-done((f32[3,2,4,1024]{3,2,1,0:T(4,128)S(1)}, f32[3,2,4,1024]{3,2,1,0:T(4,128)S(1)}, u32[]{:S(2)}, u32[]{:S(2)}) %collective-permute-start.3) | collective-permute-done | bytes 98336 | tf_op jit(solution)/shard_map/ppermute | solution.py:22
  34.5 4.3 %collective-permute-done.4 = f32[3,2,4,1024]{3,2,1,0:T(4,128)S(1)} collective-permute-done((f32[3,2,4,1024]{3,2,1,0:T(4,128)S(1)}, f32[3,2,4,1024]{3,2,1,0:T(4,128)S(1)}, u32[]{:S(2)}, u32[]{:S(2)}) %collective-permute-start.4) | collective-permute-done | bytes 98336 | tf_op jit(solution)/shard_map/ppermute | solution.py:23
  39.2 0.2 slice_multiply_fusion.5
  40.1 0.3 add_bitcast_fusion.5
  40.3 0.2 fusion.35
  40.5 0.2 fusion.4
  41.0 0.2 slice_multiply_fusion.3
  41.9 0.3 add_bitcast_fusion.3
  42.1 0.2 fusion.29
  42.3 0.2 fusion.3
  42.9 0.2 slice_multiply_fusion.1
  43.7 0.3 add_bitcast_fusion.1
  44.0 0.2 fusion.23
  44.2 0.2 fusion
  44.6 0.2 slice_multiply_fusion.13
  45.4 0.2 add_bitcast_fusion.13
  45.7 0.2 fusion.12
  46.1 0.6 %fusion.158 = (s32[1,1,1]{1,2,0:T(1,128)}, s32[1,1,1]{1,2,0:T(1,128)}) fusion(s32[1,1,2]{1,2,0:T(2,128)S(1)} %get-tuple-element.204), kind=kLoop, calls=%fused_computation.337 | loop fusion | bytes 16 | tf_op jit(solution)/shard_map/slice | solution.py:145
  50.5 3.7 %collective-permute-done.5 = f32[3,2,16,1024]{3,2,1,0:T(8,128)S(1)} collective-permute-done((f32[3,2,16,1024]{3,2,1,0:T(8,128)S(1)}, f32[3,2,16,1024]{3,2,1,0:T(8,128)S(1)}, u32[]{:S(2)}, u32[]{:S(2)}) %collective-permute-start.5) | collective-permute-done | bytes 393248 | tf_op jit(solution)/shard_map/ppermute | solution.py:31
  54.2 0.8 %pad_maximum_fusion.4 = f32[3,2,16,1024]{3,2,1,0:T(8,128)} fusion(f32[3,1,16,1024]{3,2,1,0:T(8,128)S(1)} %get-tuple-element.6, f32[3,1,16,1024]{3,2,1,0:T(8,128)S(1)} %get-tuple-element.5), kind=kLoop, calls=%fused_computation.44 | loop fusion | flops 98304 | bytes 786432 | tf_op jit(solution)/shard_map/stack | solution.py:144
  (105 shorter events, 7.1 us)
Async XLA Ops:
  0.0 12.6 %copy-start = (f32[3,2,16,1024]{3,2,1,0:T(8,128)S(1)}, f32[3,2,16,1024]{3,2,1,0:T(8,128)}, u32[]{:S(2)}) copy-start(f32[3,2,16,1024]{3,2,1,0:T(8,128)} %param.3) | copy-start | bytes 1179652
  1.1 7.1 %collective-permute-start = (f32[3,2,4,1024]{3,2,1,0:T(4,128)S(1)}, f32[3,2,4,1024]{3,2,1,0:T(4,128)S(1)}, u32[]{:S(2)}, u32[]{:S(2)}) collective-permute-start(f32[3,2,4,1024]{3,2,1,0:T(4,128)S(1)} %get-tuple-element.51), channel_id=1, source_target_pairs={{0,1},{1,2},{2,3},{4,5},{5,6},{6,7},{8,9},{9,10},{10,11},{12,13},{... | collective-permute-start | bytes 294920 | tf_op jit(solution)/shard_map/ppermute | solution.py:22
  6.1 6.5 %collective-permute-start.1 = (f32[3,2,4,1024]{3,2,1,0:T(4,128)S(1)}, f32[3,2,4,1024]{3,2,1,0:T(4,128)S(1)}, u32[]{:S(2)}, u32[]{:S(2)}) collective-permute-start(f32[3,2,4,1024]{3,2,1,0:T(4,128)S(1)} %get-tuple-element.52), channel_id=1, source_target_pairs={{1,0},{2,1},{3,2},{5,4},{6,5},{7,6},{9,8},{10,9},{11,10},{13,12},{... | collective-permute-start | bytes 294920 | tf_op jit(solution)/shard_map/ppermute | solution.py:23
  19.5 1.0 %copy-start.1 = (f32[2,2,16,1024]{3,2,1,0:T(8,128)S(1)}, f32[2,2,16,1024]{3,2,1,0:T(8,128)}, u32[]{:S(2)}) copy-start(f32[2,2,16,1024]{3,2,1,0:T(8,128)} %param.4) | copy-start | bytes 786436
  20.5 0.7 %copy-start.2 = (s32[2,8,2]{1,2,0:T(2,128)S(1)}, s32[2,8,2]{1,2,0:T(2,128)}, u32[]{:S(2)}) copy-start(s32[2,8,2]{1,2,0:T(2,128)} %param.5) | copy-start | bytes 388
  20.6 8.2 %collective-permute-start.2 = (f32[3,2,16,1024]{3,2,1,0:T(8,128)S(1)}, f32[3,2,16,1024]{3,2,1,0:T(8,128)S(1)}, u32[]{:S(2)}, u32[]{:S(2)}) collective-permute-start(f32[3,2,16,1024]{3,2,1,0:T(8,128)S(1)} %pad_maximum_fusion), channel_id=1, source_target_pairs={{0,4},{4,8},{8,12},{12,16},{16,20},{20,24},{24,28},{28,0},{1,5},{5... | collective-permute-start | bytes 1179656 | tf_op jit(solution)/shard_map/ppermute | solution.py:31
  28.8 5.7 %collective-permute-start.3 = (f32[3,2,4,1024]{3,2,1,0:T(4,128)S(1)}, f32[3,2,4,1024]{3,2,1,0:T(4,128)S(1)}, u32[]{:S(2)}, u32[]{:S(2)}) collective-permute-start(f32[3,2,4,1024]{3,2,1,0:T(4,128)S(1)} %get-tuple-element.49), channel_id=1, source_target_pairs={{0,1},{1,2},{2,3},{4,5},{5,6},{6,7},{8,9},{9,10},{10,11},{12,13},{... | collective-permute-start | bytes 294920 | tf_op jit(solution)/shard_map/ppermute | solution.py:22
  32.3 6.5 %collective-permute-start.4 = (f32[3,2,4,1024]{3,2,1,0:T(4,128)S(1)}, f32[3,2,4,1024]{3,2,1,0:T(4,128)S(1)}, u32[]{:S(2)}, u32[]{:S(2)}) collective-permute-start(f32[3,2,4,1024]{3,2,1,0:T(4,128)S(1)} %get-tuple-element.50), channel_id=1, source_target_pairs={{1,0},{2,1},{3,2},{5,4},{6,5},{7,6},{9,8},{10,9},{11,10},{13,12},{... | collective-permute-start | bytes 294920 | tf_op jit(solution)/shard_map/ppermute | solution.py:23
  46.0 8.2 %collective-permute-start.5 = (f32[3,2,16,1024]{3,2,1,0:T(8,128)S(1)}, f32[3,2,16,1024]{3,2,1,0:T(8,128)S(1)}, u32[]{:S(2)}, u32[]{:S(2)}) collective-permute-start(f32[3,2,16,1024]{3,2,1,0:T(8,128)S(1)} %pad_maximum_fusion.1), channel_id=1, source_target_pairs={{0,4},{4,8},{8,12},{12,16},{16,20},{20,24},{24,28},{28,0},{1,5},{5... | collective-permute-start | bytes 1179656 | tf_op jit(solution)/shard_map/ppermute | solution.py:31
where the time goes:
time: 55.4 us; the launch traced here: 55 us
  waiting for transfers between devices  17 us (31%)
  starting transfers between devices  11.1 us (20%)
  local copies, waits for them, and re-layouts  10.1 us (18%)
  between operations  8.48 us (15%)
  other arithmetic  8.36 us (15%)
    ppermute x2, waiting for transfers between devices, extended(): after = lax.ppermute(leading, axis, down)  8.64 us
    ppermute x2, starting transfers between devices, extended(): before = lax.ppermute(last, axis, up)  8.42 us
    ppermute x2, waiting for transfers between devices, shifted(): return lax.ppermute(value, axis, pairs)  6.68 us
    slice x46, local copies, waits for them, and re-layouts, eastward(): return jnp.roll(field_amount, -1, axis=-1)  4.36 us
    another operation x16, other arithmetic, tendency(): return jnp.stack([tend_height, tend_zonal, tend_north])  3.49 us
    ppermute x2, starting transfers between devices, extended(): after = lax.ppermute(leading, axis, down)  2.58 us
    mul x8, other arithmetic, tendency(): flux_east = column_depth[..., 1:-1, :] * zonal_mid  1.87 us
    ppermute x2, waiting for transfers between devices, extended(): before = lax.ppermute(last, axis, up)  1.65 us
  transfers between devices with their start and end apart: 6, of which 6 were waited for; matrix products, arithmetic and copies ran while one was open for 2% of the time, Pallas kernels for 0%

commit v1 on v0

v1 whole, which is shorter than its diff:
```python
import functools

import jax
import jax.numpy as jnp
from jax import lax
from jax.experimental import pallas as pl
from jax.experimental.pallas import tpu as pltpu
from jax.sharding import PartitionSpec as P

STEPS = 2
FILTER_ROUNDS = 2

time_step = 0.2
viscosity = 0.05
rotation = 0.3

LANES = 128
TILE = 8
NEAR = 2 * STEPS
HALO = NEAR * FILTER_ROUNDS
VMEM_LIMIT = 16 << 20

diffuse = time_step * viscosity
half = 0.5 * time_step
gravity = half * half
keep = 1.0 - 4.0 * diffuse


def row_tiles(value):
    lead, (rows, columns) = value.shape[:-2], value.shape[-2:]
    blocks = columns // LANES
    value = value.reshape(*lead, rows // TILE, TILE, blocks, LANES)
    return jnp.swapaxes(value, -3, -2).reshape(*lead, rows // TILE, blocks * TILE, LANES)


def from_row_tiles(value):
    lead, (tiles, sublanes) = value.shape[:-3], value.shape[-3:-1]
    blocks = sublanes // TILE
    value = jnp.swapaxes(value.reshape(*lead, tiles, blocks, TILE, LANES), -3, -2)
    return value.reshape(*lead, tiles * TILE, blocks * LANES)


def entries(table, cycle, island):
    lane = lax.broadcasted_iota(jnp.int32, table.shape[2:], 0)[None]
    first, second = (
        jnp.sum(jnp.where(lane == island, table[cycle, slot : slot + 1].astype(jnp.float32), 0.0))
        for slot in range(2)
    )
    return (
        jnp.minimum(first, second).astype(jnp.int32),
        jnp.maximum(first, second).astype(jnp.int32),
        (second > first).astype(jnp.int32),
    )


def prepare(state_ref, noise_ref, table_ref, main, xa, xb, ka, kb, kmain, later, *, islands):
    slots, tiles = state_ref.shape[1], state_ref.shape[2]
    rows = tiles * TILE
    blocks = state_ref.shape[3] // TILE
    island = lax.axis_index("dom")
    odd = lax.rem(lax.axis_index("lat"), 2)
    table = table_ref[...]
    _, wanted, _ = entries(table, 0, lax.rem(island + 1, islands))
    kept, _, _ = entries(table, 0, island)
    sent = jnp.clip(wanted - slots, 0, slots - 1)
    kept = jnp.clip(kept, 0, slots - 1)

    def state_row(field, slot, tile, row):
        value = state_ref[field, slot, tile, pl.ds(row, blocks, stride=TILE), :]
        return value if field == 0 else value * half

    def noise_row(cycle, slot, tile, row):
        return noise_ref[cycle, slot, tile, pl.ds(row, blocks, stride=TILE), :]

    for slot, whole in ((sent, main), (kept, kmain)):
        for field in range(3):
            for row in range(rows):
                whole[field * rows + row] = state_row(field, slot, row // TILE, row % TILE)
        for row in range(rows):
            whole[3 * rows + row] = noise_row(0, slot, row // TILE, row % TILE)
    for slot, edge, bottom in ((sent, xa, 1 - odd), (sent, xb, odd), (kept, ka, 1 - odd), (kept, kb, odd)):
        tile = bottom * (tiles - 1)
        for field in range(3):
            for row in range(HALO):
                edge[field * HALO + row] = state_row(field, slot, tile, row)
        for row in range(NEAR):
            edge[3 * HALO + row] = noise_row(0, slot, tile, bottom * (TILE - NEAR) + row)
    for slot in range(slots):
        for row in range(rows):
            later[slot * rows + row] = noise_row(1, slot, row // TILE, row % TILE)


def tendency_rows(load, store, first, last, coriolis):
    blocks = load(0, first).shape[0]
    lane = lax.broadcasted_iota(jnp.int32, (blocks, LANES), 1)
    at_end, at_start = lane == LANES - 1, lane == 0

    def east(value):
        turned = pltpu.roll(value, LANES - 1, 1)
        return jnp.where(at_end, pltpu.roll(turned, blocks - 1, 0), turned)

    def west(value):
        turned = pltpu.roll(value, 1, 1)
        return jnp.where(at_start, pltpu.roll(turned, 1, 0), turned)

    def column(row):
        h, u, v = (load(field, row) for field in range(3))
        minus, plus = diffuse - v, diffuse + v
        return h, u, v, minus, plus, h * minus - v, h * plus + v

    below, here = column(first - 1), column(first)
    for row in range(first, last):
        above = column(row + 1)
        h, u, v, v_minus, v_plus, _, _ = here
        h_east, h_west, u_east, u_west, v_east, v_west = east(h), west(h), east(u), west(u), east(v), west(v)
        u_minus, u_plus = diffuse - u, diffuse + u
        turn = coriolis(row)
        h_new = (
            (keep * h + (h_east * (diffuse - u_east) - u_east))
            + (h_west * (diffuse + u_west) + u_west)
            + (above[5] + below[6])
        )
        u_new = (
            (keep * u + u_east * u_minus)
            + (u_west * u_plus + above[1] * v_minus)
            + (below[1] * v_plus + turn * v)
            - gravity * (h_east - h_west)
        )
        v_new = (
            (keep * v + v_east * u_minus)
            + (v_west * u_plus + above[2] * v_minus)
            + (below[2] * v_plus - turn * u)
            - gravity * (above[0] - below[0])
        )
        store(row, h_new, u_new, v_new)
        below, here = here, above


def forecast(table_ref, main, xa, xb, kmain, ka, kb, later, out, state, middle, noise, *, islands, bands, local):
    rows = main.shape[0] // 4
    wide = rows + 2 * HALO
    island, band = lax.axis_index("dom"), lax.axis_index("lat")
    odd = lax.rem(band, 2)
    table = table_ref[...]
    _, _, foreign = entries(table, 0, island)
    if local:
        slot, _, _ = entries(table, 1, island)
    else:
        _, slot, _ = entries(table, 1, lax.rem(island + 1, islands))
        slot = slot - 2
    slot = jnp.clip(slot, 0, 1)
    arrived = slot == foreign
    inside_low = (band > 0).astype(jnp.float32)
    inside_high = (band < bands - 1).astype(jnp.float32)

    def gather(whole, first, second):
        for field in range(3):
            for row in range(rows):
                state[field * wide + HALO + row] = whole[field * rows + row]
        for row in range(rows):
            noise[NEAR + row] = whole[3 * rows + row]
        for edge, high in ((first, 1 - odd), (second, odd)):
            inside = jnp.where(high == 1, inside_high, inside_low)
            start, start_noise = high * (rows + HALO), high * (rows + NEAR)
            for field in range(3):
                for row in range(HALO):
                    state[field * wide + start + row] = edge[field * HALO + row] * inside
            for row in range(NEAR):
                noise[start_noise + row] = edge[3 * HALO + row] * inside

    @pl.when(arrived)
    def _():
        gather(main, xa, xb)

    @pl.when(jnp.logical_not(arrived))
    def _():
        gather(kmain, ka, kb)

    def within(row, value):
        if row < HALO:
            return value * inside_low
        if row >= HALO + rows:
            return value * inside_high
        return value

    start = (band * rows - HALO).astype(jnp.float32)
    slope = time_step * rotation * 2.0 / (rows * bands)
    base = slope * (start + 0.5) - time_step * rotation

    def coriolis(row):
        return base + slope * row

    margin = 0
    for cycle in range(FILTER_ROUNDS):
        for step in range(STEPS):
            last = step == STEPS - 1

            def to_middle(row, *values):
                for field, value in enumerate(values):
                    middle[field * wide + row] = within(row, value)

            def to_state(row, *values, cycle=cycle, last=last):
                final = last and cycle == FILTER_ROUNDS - 1
                for field, value in enumerate(values):
                    value = within(row, 0.5 * (state[field * wide + row] + value))
                    if last and field == 0:
                        if cycle == 0:
                            value = value + noise[row - HALO + NEAR]
                        else:
                            value = value + later[slot * rows + row - HALO]
                    if final:
                        out[field * rows + row - HALO] = value if field == 0 else value * (1.0 / half)
                    else:
                        state[field * wide + row] = value

            margin += 1
            tendency_rows(lambda field, row: state[field * wide + row], to_middle, margin, wide - margin, coriolis)
            margin += 1
            tendency_rows(lambda field, row: middle[field * wide + row], to_state, margin, wide - margin, coriolis)


def finish(table_ref, kept, arrived, out):
    rows = kept.shape[0] // 3
    blocks = out.shape[3] // TILE
    _, _, foreign = entries(table_ref[...], 1, lax.axis_index("dom"))
    for source, slot in ((kept, 1 - foreign), (arrived, foreign)):
        for field in range(3):
            for row in range(rows):
                out[field, slot, row // TILE, pl.ds(row % TILE, blocks, stride=TILE), :] = source[field * rows + row]


def on_chip(kernel, shapes, count, scratch=(), flops=0):
    vmem = pl.BlockSpec(memory_space=pltpu.VMEM)
    return pl.pallas_call(
        kernel,
        out_shape=[jax.ShapeDtypeStruct(shape, jnp.float32) for shape in shapes],
        in_specs=[vmem] * count,
        out_specs=[vmem] * len(shapes),
        scratch_shapes=[pltpu.VMEM(shape, jnp.float32) for shape in scratch],
        cost_estimate=pl.CostEstimate(flops=flops, bytes_accessed=1 << 20, transcendentals=0),
        compiler_params=pltpu.CompilerParams(vmem_limit_bytes=VMEM_LIMIT),
    )


def send(value, place):
    islands, bands = lax.axis_size("dom"), lax.axis_size("lat")
    pairs = []
    for island in range(islands):
        for band in range(bands):
            to_island, to_band = place(island, band)
            pairs.append((island * bands + band, to_island * bands + to_band))
    return lax.ppermute(value, ("dom", "lat"), pairs)


def body(states, stir_noise, ancestors):
    islands, bands = lax.axis_size("dom"), lax.axis_size("lat")
    rows, columns = states.shape[2:]
    blocks = columns // LANES
    wide = rows + 2 * HALO
    state_tiles, noise_tiles = row_tiles(states), row_tiles(stir_noise)
    table = jnp.swapaxes(ancestors, 1, 2)

    def pair(band, turn):
        partner = band + 1 if band % 2 == turn else band - 1
        return partner if 0 <= partner < bands else None

    def following(island, band):
        return (island + 1) % islands, band

    def across(turn, step):
        def place(island, band):
            partner = pair(band, turn)
            if partner is not None:
                return (island + step) % islands, partner
            if step:
                return (island + step) % islands, band
            return (island ^ 1 if islands % 2 == 0 else (island + 1) % islands), band

        return place

    full, edge = (4 * rows, blocks, LANES), (3 * HALO + NEAR, blocks, LANES)
    later_shape = (states.shape[1] * rows, blocks, LANES)
    main, xa, xb, ka, kb, kmain, later = on_chip(
        functools.partial(prepare, islands=islands), [full, edge, edge, edge, edge, full, later_shape], 3
    )(state_tiles, noise_tiles, table)
    main = send(main, following)
    xa, xb = send(xa, across(0, 1)), send(xb, across(1, 1))
    ka, kb = send(ka, across(0, 0)), send(kb, across(1, 0))

    scratch = [(3 * wide, blocks, LANES)] * 2 + [(rows + 2 * NEAR, blocks, LANES)]
    result = (3 * rows, blocks, LANES)
    flops = 60 * wide * columns * 4 * STEPS

    def run(local):
        kernel = functools.partial(forecast, islands=islands, bands=bands, local=local)
        (value,) = on_chip(kernel, [result], 8, scratch, flops)(table, main, xa, xb, kmain, ka, kb, later)
        return value

    arrived = send(run(False), following)
    kept = run(True)
    (out,) = on_chip(finish, [(3,) + state_tiles.shape[1:]], 3)(table, kept, arrived)
    return from_row_tiles(out)


def solution(mesh):
    in_specs = (P(None, "dom", "lat", None), P(None, "dom", "lat", None), P())
    out_specs = P(None, "dom", "lat", None)
    return jax.shard_map(body, mesh=mesh, in_specs=in_specs, out_specs=out_specs, check_vma=False)
```

time: 55.4 us -> 22.6 us (0.41)
  the two profiles are of different devices: /device:TPU:0 before, /device:TPU:20 now
where the time goes in v1:
time: 22.6 us; the launch traced here: 22.4 us
  waiting for transfers between devices  10.5 us (46%)
  Pallas kernels  4.89 us (22%)
  starting transfers between devices  4.42 us (20%)
  local copies, waits for them, and re-layouts  2.63 us (12%)
    ppermute x6, waiting for transfers between devices, send(): return lax.ppermute(value, ('dom', 'lat'), pairs)  10.5 us
    ppermute x6, starting transfers between devices, send(): return lax.ppermute(value, ('dom', 'lat'), pairs)  4.42 us
    pallas_call x2, Pallas kernels, run(): on_chip(kernel, [result], 8, scratch, flops)  3.61 us
    unnamed x6, local copies, waits for them, and re-layouts  2.63 us
    pallas_call x1, Pallas kernels, body(): on_chip(finish, [(3,) + state_tiles.shape[1:]], 3)(table, kept, arrived)  0.93 us
  transfers between devices with their start and end apart: 6, of which 4 were waited for; matrix products, arithmetic and copies ran while one was open for 0% of the time, Pallas kernels for 8%

profile of v1, /device:TPU:20, one launch (start us, length us, event | category | flops | bytes accessed | tf_op | source)
XLA Modules:
  0.0 22.4 jit_solution(7435854309278636073)
XLA Ops:
  0.0 0.0 copy-start.2
  0.0 0.7 %copy-done.2 = s32[2,8,2]{1,2,0:T(2,128)S(1)} copy-done((s32[2,8,2]{1,2,0:T(2,128)S(1)}, s32[2,8,2]{1,2,0:T(2,128)}, u32[]{:S(2)}) %copy-start.2) | copy-done | bytes 152
  0.7 0.0 copy-start
  0.7 1.0 %copy-done = f32[3,2,16,1024]{3,2,1,0:T(8,128)S(1)} copy-done((f32[3,2,16,1024]{3,2,1,0:T(8,128)S(1)}, f32[3,2,16,1024]{3,2,1,0:T(8,128)}, u32[]{:S(2)}) %copy-start) | copy-done | bytes 393240
  1.7 0.0 copy-start.1
  1.7 0.9 %copy-done.1 = f32[2,2,16,1024]{3,2,1,0:T(8,128)S(1)} copy-done((f32[2,2,16,1024]{3,2,1,0:T(8,128)S(1)}, f32[2,2,16,1024]{3,2,1,0:T(8,128)}, u32[]{:S(2)}) %copy-start.1) | copy-done | bytes 262168
  2.6 0.4 %shard_map.37 = (f32[64,8,128]{2,1,0:T(8,128)S(1)}, f32[28,8,128]{2,1,0:T(8,128)S(1)}, f32[28,8,128]{2,1,0:T(8,128)S(1)}, f32[28,8,128]{2,1,0:T(8,128)S(1)}, f32...) custom-call(f32[3,2,2,64,128]{4,3,2,1,0:T(8,128)S(1)} %bitcast.16, ...), custom_call_target="tpu_custom_call" | custom-call | bytes 1048576 | tf_op jit(solution)/shard_map/pallas_call | solution.py:283
  3.0 0.1 collective-permute-start
  3.1 2.8 %collective-permute-start.1 = (f32[28,8,128]{2,1,0:T(8,128)S(1)}, f32[28,8,128]{2,1,0:T(8,128)S(1)}, u32[]{:S(2)}, u32[]{:S(2)}) collective-permute-start(f32[28,8,128]{2,1,0:T(8,128)S(1)} %get-tuple-element.13), channel_id=1, source_target_pairs={{0,5},{1,4},{2,7},{3,6},{4,9},{5,8},{6,11},{7,10},{8,13},{9,12},{1... | collective-permute-start | bytes 344072 | tf_op jit(solution)/shard_map/ppermute | solution.py:252
  5.8 0.0 collective-permute-start.2
  5.8 0.4 %collective-permute-start.3 = (f32[28,8,128]{2,1,0:T(8,128)S(1)}, f32[28,8,128]{2,1,0:T(8,128)S(1)}, u32[]{:S(2)}, u32[]{:S(2)}) collective-permute-start(f32[28,8,128]{2,1,0:T(8,128)S(1)} %get-tuple-element.16), channel_id=1, source_target_pairs={{0,1},{1,0},{2,3},{3,2},{4,5},{5,4},{6,7},{7,6},{8,9},{9,8},{10,11... | collective-permute-start | bytes 344072 | tf_op jit(solution)/shard_map/ppermute | solution.py:252
  6.3 1.1 %collective-permute-start.4 = (f32[28,8,128]{2,1,0:T(8,128)S(1)}, f32[28,8,128]{2,1,0:T(8,128)S(1)}, u32[]{:S(2)}, u32[]{:S(2)}) collective-permute-start(f32[28,8,128]{2,1,0:T(8,128)S(1)} %get-tuple-element.17), channel_id=1, source_target_pairs={{0,4},{1,2},{2,1},{3,7},{4,0},{5,6},{6,5},{7,3},{8,12},{9,10},{10,... | collective-permute-start | bytes 344072 | tf_op jit(solution)/shard_map/ppermute | solution.py:252
  7.4 2.3 %collective-permute-done.1.xa = f32[28,8,128]{2,1,0:T(8,128)S(1)} collective-permute-done((f32[28,8,128]{2,1,0:T(8,128)S(1)}, f32[28,8,128]{2,1,0:T(8,128)S(1)}, u32[]{:S(2)}, u32[]{:S(2)}) %collective-permute-start.1) | collective-permute-done | bytes 114720 | tf_op jit(solution)/shard_map/ppermute | solution.py:252
  9.7 3.4 %collective-permute-done.2.xb = f32[28,8,128]{2,1,0:T(8,128)S(1)} collective-permute-done((f32[28,8,128]{2,1,0:T(8,128)S(1)}, f32[28,8,128]{2,1,0:T(8,128)S(1)}, u32[]{:S(2)}, u32[]{:S(2)}) %collective-permute-start.2) | collective-permute-done | bytes 114720 | tf_op jit(solution)/shard_map/ppermute | solution.py:252
  13.1 0.0 collective-permute-done.3.ka
  13.1 0.6 %collective-permute-done.4.kb = f32[28,8,128]{2,1,0:T(8,128)S(1)} collective-permute-done((f32[28,8,128]{2,1,0:T(8,128)S(1)}, f32[28,8,128]{2,1,0:T(8,128)S(1)}, u32[]{:S(2)}, u32[]{:S(2)}) %collective-permute-start.4) | collective-permute-done | bytes 114720 | tf_op jit(solution)/shard_map/ppermute | solution.py:252
  13.7 0.0 collective-permute-done.main
  13.7 1.8 %shard_map.39 = f32[48,8,128]{2,1,0:T(8,128)S(1)} custom-call(s32[2,2,8]{2,1,0:T(2,128)S(1)} %bitcast.19, f32[64,8,128]{2,1,0:T(8,128)S(1)} %collective-permute-done.main, f32[28,8,128]{2,1,0:T(8,128)S(1)} %collective-permute-done.1.xa, f32[28,8,128]{2,1,0:T(8,128)S(1)} %collective-permute-done.2.xb, f32[64,8,128]{2,1,0:T(8,128)S(1)} %get-tuple-element.15.kmain, ...), custom_call_target="tpu_custom_call" | custom-call | flops 15728640 | bytes 1048576 | tf_op jit(solution)/shard_map/pallas_call | solution.py:296
  15.5 0.1 collective-permute-start.5
  15.5 1.8 %shard_map.38.kept = f32[48,8,128]{2,1,0:T(8,128)S(1)} custom-call(s32[2,2,8]{2,1,0:T(2,128)S(1)} %bitcast.20, f32[64,8,128]{2,1,0:T(8,128)S(1)} %collective-permute-done.main, f32[28,8,128]{2,1,0:T(8,128)S(1)} %collective-permute-done.1.xa, f32[28,8,128]{2,1,0:T(8,128)S(1)} %collective-permute-done.2.xb, f32[64,8,128]{2,1,0:T(8,128)S(1)} %get-tuple-element.15.kmain, ...), custom_call_target="tpu_custom_call" | custom-call | flops 15728640 | bytes 1048576 | tf_op jit(solution)/shard_map/pallas_call | solution.py:296
  17.3 4.2 %collective-permute-done.5.arrived = f32[48,8,128]{2,1,0:T(8,128)S(1)} collective-permute-done((f32[48,8,128]{2,1,0:T(8,128)S(1)}, f32[48,8,128]{2,1,0:T(8,128)S(1)}, u32[]{:S(2)}, u32[]{:S(2)}) %collective-permute-start.5) | collective-permute-done | bytes 196640 | tf_op jit(solution)/shard_map/ppermute | solution.py:252
  21.5 0.9 %shard_map.40 = f32[3,2,2,64,128]{4,3,2,1,0:T(8,128)} custom-call(s32[2,2,8]{2,1,0:T(2,128)S(1)} %bitcast.21, f32[48,8,128]{2,1,0:T(8,128)S(1)} %shard_map.38.kept, f32[48,8,128]{2,1,0:T(8,128)S(1)} %collective-permute-done.5.arrived), custom_call_target="tpu_custom_call" | custom-call | bytes 1048576 | tf_op jit(solution)/shard_map/pallas_call | solution.py:301
Async XLA Ops:
  0.0 0.7 %copy-start.2 = (s32[2,8,2]{1,2,0:T(2,128)S(1)}, s32[2,8,2]{1,2,0:T(2,128)}, u32[]{:S(2)}) copy-start(s32[2,8,2]{1,2,0:T(2,128)} %param.5) | copy-start | bytes 388
  0.7 1.0 %copy-start = (f32[3,2,16,1024]{3,2,1,0:T(8,128)S(1)}, f32[3,2,16,1024]{3,2,1,0:T(8,128)}, u32[]{:S(2)}) copy-start(f32[3,2,16,1024]{3,2,1,0:T(8,128)} %param.3) | copy-start | bytes 1179652
  1.7 0.9 %copy-start.1 = (f32[2,2,16,1024]{3,2,1,0:T(8,128)S(1)}, f32[2,2,16,1024]{3,2,1,0:T(8,128)}, u32[]{:S(2)}) copy-start(f32[2,2,16,1024]{3,2,1,0:T(8,128)} %param.4) | copy-start | bytes 786436
  3.0 10.7 %collective-permute-start = (f32[64,8,128]{2,1,0:T(8,128)S(1)}, f32[64,8,128]{2,1,0:T(8,128)S(1)}, u32[]{:S(2)}, u32[]{:S(2)}) collective-permute-start(f32[64,8,128]{2,1,0:T(8,128)S(1)} %get-tuple-element.12), channel_id=1, source_target_pairs={{0,4},{1,5},{2,6},{3,7},{4,8},{5,9},{6,10},{7,11},{8,12},{9,13},{1... | collective-permute-start | bytes 786440 | tf_op jit(solution)/shard_map/ppermute | solution.py:252
  3.1 6.6 %collective-permute-start.1 = (f32[28,8,128]{2,1,0:T(8,128)S(1)}, f32[28,8,128]{2,1,0:T(8,128)S(1)}, u32[]{:S(2)}, u32[]{:S(2)}) collective-permute-start(f32[28,8,128]{2,1,0:T(8,128)S(1)} %get-tuple-element.13), channel_id=1, source_target_pairs={{0,5},{1,4},{2,7},{3,6},{4,9},{5,8},{6,11},{7,10},{8,13},{9,12},{1... | collective-permute-start | bytes 344072 | tf_op jit(solution)/shard_map/ppermute | solution.py:252
  5.8 7.2 %collective-permute-start.2 = (f32[28,8,128]{2,1,0:T(8,128)S(1)}, f32[28,8,128]{2,1,0:T(8,128)S(1)}, u32[]{:S(2)}, u32[]{:S(2)}) collective-permute-start(f32[28,8,128]{2,1,0:T(8,128)S(1)} %get-tuple-element.14), channel_id=1, source_target_pairs={{0,4},{1,6},{2,5},{3,7},{4,8},{5,10},{6,9},{7,11},{8,12},{9,14},{1... | collective-permute-start | bytes 344072 | tf_op jit(solution)/shard_map/ppermute | solution.py:252
  5.8 7.2 %collective-permute-start.3 = (f32[28,8,128]{2,1,0:T(8,128)S(1)}, f32[28,8,128]{2,1,0:T(8,128)S(1)}, u32[]{:S(2)}, u32[]{:S(2)}) collective-permute-start(f32[28,8,128]{2,1,0:T(8,128)S(1)} %get-tuple-element.16), channel_id=1, source_target_pairs={{0,1},{1,0},{2,3},{3,2},{4,5},{5,4},{6,7},{7,6},{8,9},{9,8},{10,11... | collective-permute-start | bytes 344072 | tf_op jit(solution)/shard_map/ppermute | solution.py:252
  6.3 7.4 %collective-permute-start.4 = (f32[28,8,128]{2,1,0:T(8,128)S(1)}, f32[28,8,128]{2,1,0:T(8,128)S(1)}, u32[]{:S(2)}, u32[]{:S(2)}) collective-permute-start(f32[28,8,128]{2,1,0:T(8,128)S(1)} %get-tuple-element.17), channel_id=1, source_target_pairs={{0,4},{1,2},{2,1},{3,7},{4,0},{5,6},{6,5},{7,3},{8,12},{9,10},{10,... | collective-permute-start | bytes 344072 | tf_op jit(solution)/shard_map/ppermute | solution.py:252
  15.5 6.0 %collective-permute-start.5 = (f32[48,8,128]{2,1,0:T(8,128)S(1)}, f32[48,8,128]{2,1,0:T(8,128)S(1)}, u32[]{:S(2)}, u32[]{:S(2)}) collective-permute-start(f32[48,8,128]{2,1,0:T(8,128)S(1)} %shard_map.39), channel_id=1, source_target_pairs={{0,4},{1,5},{2,6},{3,7},{4,8},{5,9},{6,10},{7,11},{8,12},{9,13},{1... | collective-permute-start | bytes 589832 | tf_op jit(solution)/shard_map/ppermute | solution.py:252

commit v2 on v1

--- a/solution.py
+++ b/solution.py
@@ -53,10 +53,44 @@
     )
 
 
-def prepare(state_ref, noise_ref, table_ref, main, xa, xb, ka, kb, kmain, later, *, islands):
+def collect(state_hbm, noise_hbm, table_hbm, main, state_ref, noise_ref, table_ref, done, *, islands):
+    copies = [
+        pltpu.make_async_copy(source, target, done.at[index])
+        for index, (source, target) in enumerate(
+            ((table_hbm, table_ref), (state_hbm, state_ref), (noise_hbm.at[0], noise_ref.at[0]), (noise_hbm.at[1], noise_ref.at[1]))
+        )
+    ]
+    for copy in copies:
+        copy.start()
     slots, tiles = state_ref.shape[1], state_ref.shape[2]
     rows = tiles * TILE
+    copies[0].wait()
+    _, wanted, _ = entries(table_ref[...], 0, lax.rem(lax.axis_index("dom") + 1, islands))
+    sent = jnp.clip(wanted - slots, 0, slots - 1)
+    copies[1].wait()
+    for field in range(3):
+        for row in range(rows):
+            main[field * rows + row] = state_row(state_ref, field, sent, row // TILE, row % TILE)
+    copies[2].wait()
+    for row in range(rows):
+        main[3 * rows + row] = noise_row(noise_ref, 0, sent, row // TILE, row % TILE)
+    copies[3].wait()
+
+
+def state_row(state_ref, field, slot, tile, row):
     blocks = state_ref.shape[3] // TILE
+    value = state_ref[field, slot, tile, pl.ds(row, blocks, stride=TILE), :]
+    return value if field == 0 else value * half
+
+
+def noise_row(noise_ref, cycle, slot, tile, row):
+    blocks = noise_ref.shape[3] // TILE
+    return noise_ref[cycle, slot, tile, pl.ds(row, blocks, stride=TILE), :]
+
+
+def edges(state_ref, noise_ref, table_ref, xa, xb, ka, kb, kmain, later, *, islands):
+    slots, tiles = state_ref.shape[1], state_ref.shape[2]
+    rows = tiles * TILE
     island = lax.axis_index("dom")
     odd = lax.rem(lax.axis_index("lat"), 2)
     table = table_ref[...]
@@ -64,30 +98,21 @@
     kept, _, _ = entries(table, 0, island)
     sent = jnp.clip(wanted - slots, 0, slots - 1)
     kept = jnp.clip(kept, 0, slots - 1)
-
-    def state_row(field, slot, tile, row):
-        value = state_ref[field, slot, tile, pl.ds(row, blocks, stride=TILE), :]
-        return value if field == 0 else value * half
-
-    def noise_row(cycle, slot, tile, row):
-        return noise_ref[cycle, slot, tile, pl.ds(row, blocks, stride=TILE), :]
-
-    for slot, whole in ((sent, main), (kept, kmain)):
-        for field in range(3):
-            for row in range(rows):
-                whole[field * rows + row] = state_row(field, slot, row // TILE, row % TILE)
-        for row in range(rows):
-            whole[3 * rows + row] = noise_row(0, slot, row // TILE, row % TILE)
     for slot, edge, bottom in ((sent, xa, 1 - odd), (sent, xb, odd), (kept, ka, 1 - odd), (kept, kb, odd)):
         tile = bottom * (tiles - 1)
         for field in range(3):
             for row in range(HALO):
-                edge[field * HALO + row] = state_row(field, slot, tile, row)
+                edge[field * HALO + row] = state_row(state_ref, field, slot, tile, row)
         for row in range(NEAR):
-            edge[3 * HALO + row] = noise_row(0, slot, tile, bottom * (TILE - NEAR) + row)
+            edge[3 * HALO + row] = noise_row(noise_ref, 0, slot, tile, bottom * (TILE - NEAR) + row)
+    for field in range(3):
+        for row in range(rows):
+            kmain[field * rows + row] = state_row(state_ref, field, kept, row // TILE, row % TILE)
+    for row in range(rows):
+        kmain[3 * rows + row] = noise_row(noise_ref, 0, kept, row // TILE, row % TILE)
     for slot in range(slots):
         for row in range(rows):
-            later[slot * rows + row] = noise_row(1, slot, row // TILE, row % TILE)
+            later[slot * rows + row] = noise_row(noise_ref, 1, slot, row // TILE, row % TILE)
 
 
 def tendency_rows(load, store, first, last, coriolis):
@@ -136,18 +161,14 @@
         below, here = here, above
 
 
-def forecast(table_ref, main, xa, xb, kmain, ka, kb, later, out, state, middle, noise, *, islands, bands, local):
+def forecast(slot, table, sources, out, state, middle, noise, bands):
+    main, xa, xb, kmain, ka, kb, later = sources
     rows = main.shape[0] // 4
+    blocks = main.shape[1]
     wide = rows + 2 * HALO
     island, band = lax.axis_index("dom"), lax.axis_index("lat")
     odd = lax.rem(band, 2)
-    table = table_ref[...]
     _, _, foreign = entries(table, 0, island)
-    if local:
-        slot, _, _ = entries(table, 1, island)
-    else:
-        _, slot, _ = entries(table, 1, lax.rem(island + 1, islands))
-        slot = slot - 2
     slot = jnp.clip(slot, 0, 1)
     arrived = slot == foreign
     inside_low = (band > 0).astype(jnp.float32)
@@ -209,7 +230,9 @@
                         else:
                             value = value + later[slot * rows + row - HALO]
                     if final:
-                        out[field * rows + row - HALO] = value if field == 0 else value * (1.0 / half)
+                        own = row - HALO
+                        value = value if field == 0 else value * (1.0 / half)
+                        out[field, own // TILE, pl.ds(own % TILE, blocks, stride=TILE), :] = value
                     else:
                         state[field * wide + row] = value
 
@@ -219,26 +242,81 @@
             tendency_rows(lambda field, row: middle[field * wide + row], to_state, margin, wide - margin, coriolis)
 
 
-def finish(table_ref, kept, arrived, out):
-    rows = kept.shape[0] // 3
-    blocks = out.shape[3] // TILE
+def wanted_slot(table, islands):
+    _, slot, _ = entries(table, 1, lax.rem(lax.axis_index("dom") + 1, islands))
+    return slot - 2
+
+
+def kept_slot(table):
+    slot, _, _ = entries(table, 1, lax.axis_index("dom"))
+    return slot
+
+
+def odd_island():
+    return lax.rem(lax.axis_index("dom"), 2)
+
+
+def payload_odd(table_ref, *refs, islands, bands):
+    *sources, out, state, middle, noise = refs
+
+    @pl.when(odd_island() == 1)
+    def _():
+        table = table_ref[...]
+        forecast(wanted_slot(table, islands), table, sources, out, state, middle, noise, bands)
+
+
+def payload_even(table_ref, *refs, islands, bands):
+    *sources, out, state, middle, noise = refs
+    table = table_ref[...]
+    slot = jnp.where(odd_island() == 1, kept_slot(table), wanted_slot(table, islands))
+    forecast(slot, table, sources, out, state, middle, noise, bands)
+
+
+def keep_local(table_ref, *refs, bands):
+    *sources, out, state, middle, noise = refs
+
+    @pl.when(odd_island() == 0)
+    def _():
+        table = table_ref[...]
+        forecast(kept_slot(table), table, sources, out, state, middle, noise, bands)
+
+
+def finish(table_ref, far, second, near, third, out, done):
     _, _, foreign = entries(table_ref[...], 1, lax.axis_index("dom"))
-    for source, slot in ((kept, 1 - foreign), (arrived, foreign)):
-        for field in range(3):
-            for row in range(rows):
-                out[field, slot, row // TILE, pl.ds(row % TILE, blocks, stride=TILE), :] = source[field * rows + row]
-
-
-def on_chip(kernel, shapes, count, scratch=(), flops=0):
-    vmem = pl.BlockSpec(memory_space=pltpu.VMEM)
+
+    def write(kept, taken):
+        copies = [
+            pltpu.make_async_copy(kept, out.at[:, 1 - foreign], done.at[0]),
+            pltpu.make_async_copy(taken, out.at[:, foreign], done.at[1]),
+        ]
+        for copy in copies:
+            copy.start()
+        for copy in copies:
+            copy.wait()
+
+    @pl.when(odd_island() == 1)
+    def _():
+        write(second, near)
+
+    @pl.when(odd_island() == 0)
+    def _():
+        write(third, far)
+
+
+VMEM = pl.BlockSpec(memory_space=pltpu.VMEM)
+HBM = pl.BlockSpec(memory_space=pltpu.HBM)
+
+
+def on_chip(kernel, ins, outs, scratch=(), flops=0, **more):
     return pl.pallas_call(
         kernel,
-        out_shape=[jax.ShapeDtypeStruct(shape, jnp.float32) for shape in shapes],
-        in_specs=[vmem] * count,
-        out_specs=[vmem] * len(shapes),
-        scratch_shapes=[pltpu.VMEM(shape, jnp.float32) for shape in scratch],
+        in_specs=ins,
+        out_shape=[jax.ShapeDtypeStruct(shape, dtype) for _, shape, dtype in outs],
+        out_specs=[spec for spec, _, _ in outs],
+        scratch_shapes=scratch,
         cost_estimate=pl.CostEstimate(flops=flops, bytes_accessed=1 << 20, transcendentals=0),
         compiler_params=pltpu.CompilerParams(vmem_limit_bytes=VMEM_LIMIT),
+        **more,
     )
 
 
@@ -252,6 +330,9 @@
     return lax.ppermute(value, ("dom", "lat"), pairs)
 
 
+ORDER = ("main", "xa", "xb", "ka", "kb")
+
+
 def body(states, stir_noise, ancestors):
     islands, bands = lax.axis_size("dom"), lax.axis_size("lat")
     rows, columns = states.shape[2:]
@@ -267,38 +348,55 @@
     def following(island, band):
         return (island + 1) % islands, band
 
+    def beside(island, band):
+        return (island ^ 1 if islands % 2 == 0 else (island + 1) % islands), band
+
     def across(turn, step):
         def place(island, band):
             partner = pair(band, turn)
             if partner is not None:
                 return (island + step) % islands, partner
-            if step:
-                return (island + step) % islands, band
-            return (island ^ 1 if islands % 2 == 0 else (island + 1) % islands), band
+            return ((island + step) % islands, band) if step else beside(island, band)
 
         return place
 
-    full, edge = (4 * rows, blocks, LANES), (3 * HALO + NEAR, blocks, LANES)
-    later_shape = (states.shape[1] * rows, blocks, LANES)
-    main, xa, xb, ka, kb, kmain, later = on_chip(
-        functools.partial(prepare, islands=islands), [full, edge, edge, edge, edge, full, later_shape], 3
+    real = jnp.float32
+    full, edge = (VMEM, (4 * rows, blocks, LANES), real), (VMEM, (3 * HALO + NEAR, blocks, LANES), real)
+    later_rows = (VMEM, (states.shape[1] * rows, blocks, LANES), real)
+    sends = {}
+    sends["main"], state_tiles, noise_tiles, table = on_chip(
+        functools.partial(collect, islands=islands),
+        [HBM] * 3,
+        [full, (VMEM, state_tiles.shape, real), (VMEM, noise_tiles.shape, real), (VMEM, table.shape, jnp.int32)],
+        [pltpu.SemaphoreType.DMA((4,))],
+    )(*(pltpu.with_memory_space_constraint(value, pltpu.HBM) for value in (state_tiles, noise_tiles, table)))
+    sends["xa"], sends["xb"], sends["ka"], sends["kb"], kmain, later = on_chip(
+        functools.partial(edges, islands=islands), [VMEM] * 3, [edge] * 4 + [full, later_rows]
     )(state_tiles, noise_tiles, table)
-    main = send(main, following)
-    xa, xb = send(xa, across(0, 1)), send(xb, across(1, 1))
-    ka, kb = send(ka, across(0, 0)), send(kb, across(1, 0))
-
-    scratch = [(3 * wide, blocks, LANES)] * 2 + [(rows + 2 * NEAR, blocks, LANES)]
-    result = (3 * rows, blocks, LANES)
+    places = {
+        "main": following,
+        "xa": across(0, 1),
+        "xb": across(1, 1),
+        "ka": across(0, 0),
+        "kb": across(1, 0),
+    }
+    got = {name: send(sends[name], places[name]) for name in ORDER}
+    sources = (table, got["main"], got["xa"], got["xb"], kmain, got["ka"], got["kb"], later)
+
+    work = [pltpu.VMEM((3 * wide, blocks, LANES), real)] * 2 + [pltpu.VMEM((rows + 2 * NEAR, blocks, LANES), real)]
+    result = (3,) + state_tiles.shape[2:]
     flops = 60 * wide * columns * 4 * STEPS
-
-    def run(local):
-        kernel = functools.partial(forecast, islands=islands, bands=bands, local=local)
-        (value,) = on_chip(kernel, [result], 8, scratch, flops)(table, main, xa, xb, kmain, ka, kb, later)
-        return value
-
-    arrived = send(run(False), following)
-    kept = run(True)
-    (out,) = on_chip(finish, [(3,) + state_tiles.shape[1:]], 3)(table, kept, arrived)
+    sizes = dict(islands=islands, bands=bands)
+    (first,) = on_chip(functools.partial(payload_odd, **sizes), [VMEM] * 8, [(VMEM, result, real)], work, flops)(*sources)
+    far = send(first, following)
+    (second,) = on_chip(functools.partial(payload_even, **sizes), [VMEM] * 8, [(VMEM, result, real)], work, flops)(*sources)
+    near = send(second, beside)
+    (third,) = on_chip(functools.partial(keep_local, bands=bands), [VMEM] * 8, [(VMEM, result, real)], work, flops)(
+        *sources
+    )
+    (out,) = on_chip(
+        finish, [VMEM] * 5, [(HBM, state_tiles.shape, real)], [pltpu.SemaphoreType.DMA((2,))]
+    )(table, far, second, near, third)
     return from_row_tiles(out)
 
 

time: 22.6 us -> 19.5 us (0.86)
  the two profiles are of different devices: /device:TPU:20 before, /device:TPU:0 now
where the time goes in v2:
time: 19.5 us; the launch traced here: 19.4 us
  starting transfers between devices  10.9 us (56%)
  Pallas kernels  5.94 us (30%)
  waiting for transfers between devices  2.5 us (13%)
    ppermute x7, starting transfers between devices, send(): return lax.ppermute(value, ('dom', 'lat'), pairs)  10.9 us
    ppermute x7, waiting for transfers between devices, send(): return lax.ppermute(value, ('dom', 'lat'), pairs)  2.5 us
    pallas_call x1, Pallas kernels, body(): on_chip(functools.partial(payload_even, **sizes), [VMEM] * 8, [(VMEM, res...  1.81 us
    pallas_call x1, Pallas kernels, body(): on_chip(functools.partial(keep_local, bands=bands), [VMEM] * 8, [(VMEM, r...  1.81 us
    pallas_call x1, Pallas kernels, body(): on_chip(functools.partial(collect, islands=islands), [HBM] * 3, [full, (V...  1.13 us
    pallas_call x1, Pallas kernels, body(): on_chip(finish, [VMEM] * 5, [(HBM, state_tiles.shape, real)], [pltpu.Sema...  0.89 us
  transfers between devices with their start and end apart: 7, of which 4 were waited for; matrix products, arithmetic and copies ran while one was open for 0% of the time, Pallas kernels for 20%

profile of v2, /device:TPU:0, one launch (start us, length us, event | category | flops | bytes accessed | tf_op | source)
XLA Modules:
  0.0 19.4 jit_solution(8282179989389035747)
XLA Ops:
  0.0 1.1 %shard_map.37 = (f32[64,8,128]{2,1,0:T(8,128)S(1)}, f32[3,2,2,64,128]{4,3,2,1,0:T(8,128)S(1)}, f32[2,2,2,64,128]{4,3,2,1,0:T(8,128)S(1)}, s32[2,2,8]{2,1,0:T(2,128)S(1)}) custom-call(f32[3,2,2,64,128]{4,3,2,1,0:T(8,128)} %bitcast.16, f32[2,2,2,64,128]{4,3,2,1,0:T(8,128)} %bitcast.17, s32[2,2,8]{2,1,0:T(2,128)} %bitcast.18), custom_call_target="tpu_custom_call" | custom-call | bytes 1048576 | tf_op jit(solution)/shard_map/pallas_call | solution.py:367
  1.1 0.5 %collective-permute-start = (f32[64,8,128]{2,1,0:T(8,128)S(1)}, f32[64,8,128]{2,1,0:T(8,128)S(1)}, u32[]{:S(2)}, u32[]{:S(2)}) collective-permute-start(f32[64,8,128]{2,1,0:T(8,128)S(1)} %get-tuple-element.16), channel_id=1, source_target_pairs={{0,4},{1,5},{2,6},{3,7},{4,8},{5,9},{6,10},{7,11},{8,12},{9,13},{1... | collective-permute-start | bytes 786440 | tf_op jit(solution)/shard_map/ppermute | solution.py:330
  1.6 0.3 %shard_map.38 = (f32[28,8,128]{2,1,0:T(8,128)S(1)}, f32[28,8,128]{2,1,0:T(8,128)S(1)}, f32[28,8,128]{2,1,0:T(8,128)S(1)}, f32[28,8,128]{2,1,0:T(8,128)S(1)}, f32...) custom-call(f32[3,2,2,64,128]{4,3,2,1,0:T(8,128)S(1)} %get-tuple-element.17.state_ref, ...), custom_call_target="tpu_custom_call" | custom-call | bytes 1048576 | tf_op jit(solution)/shard_map/pallas_call | solution.py:373
  2.0 3.8 %collective-permute-start.1 = (f32[28,8,128]{2,1,0:T(8,128)S(1)}, f32[28,8,128]{2,1,0:T(8,128)S(1)}, u32[]{:S(2)}, u32[]{:S(2)}) collective-permute-start(f32[28,8,128]{2,1,0:T(8,128)S(1)} %get-tuple-element.19), channel_id=1, source_target_pairs={{0,5},{1,4},{2,7},{3,6},{4,9},{5,8},{6,11},{7,10},{8,13},{9,12},{1... | collective-permute-start | bytes 344072 | tf_op jit(solution)/shard_map/ppermute | solution.py:330
  5.8 0.0 collective-permute-start.2
  5.8 2.6 %collective-permute-start.3 = (f32[28,8,128]{2,1,0:T(8,128)S(1)}, f32[28,8,128]{2,1,0:T(8,128)S(1)}, u32[]{:S(2)}, u32[]{:S(2)}) collective-permute-start(f32[28,8,128]{2,1,0:T(8,128)S(1)} %get-tuple-element.22), channel_id=1, source_target_pairs={{0,1},{1,0},{2,3},{3,2},{4,5},{5,4},{6,7},{7,6},{8,9},{9,8},{10,11... | collective-permute-start | bytes 344072 | tf_op jit(solution)/shard_map/ppermute | solution.py:330
  8.4 1.3 %collective-permute-start.4 = (f32[28,8,128]{2,1,0:T(8,128)S(1)}, f32[28,8,128]{2,1,0:T(8,128)S(1)}, u32[]{:S(2)}, u32[]{:S(2)}) collective-permute-start(f32[28,8,128]{2,1,0:T(8,128)S(1)} %get-tuple-element.23), channel_id=1, source_target_pairs={{0,4},{1,2},{2,1},{3,7},{4,0},{5,6},{6,5},{7,3},{8,12},{9,10},{10,... | collective-permute-start | bytes 344072 | tf_op jit(solution)/shard_map/ppermute | solution.py:330
  9.7 0.5 %collective-permute-done.1.refs_1_ = f32[28,8,128]{2,1,0:T(8,128)S(1)} collective-permute-done((f32[28,8,128]{2,1,0:T(8,128)S(1)}, f32[28,8,128]{2,1,0:T(8,128)S(1)}, u32[]{:S(2)}, u32[]{:S(2)}) %collective-permute-start.1) | collective-permute-done | bytes 114720 | tf_op jit(solution)/shard_map/ppermute | solution.py:330
  10.2 0.9 %collective-permute-done.2.refs_2_ = f32[28,8,128]{2,1,0:T(8,128)S(1)} collective-permute-done((f32[28,8,128]{2,1,0:T(8,128)S(1)}, f32[28,8,128]{2,1,0:T(8,128)S(1)}, u32[]{:S(2)}, u32[]{:S(2)}) %collective-permute-start.2) | collective-permute-done | bytes 114720 | tf_op jit(solution)/shard_map/ppermute | solution.py:330
  11.2 0.3 %collective-permute-done.3.refs_4_ = f32[28,8,128]{2,1,0:T(8,128)S(1)} collective-permute-done((f32[28,8,128]{2,1,0:T(8,128)S(1)}, f32[28,8,128]{2,1,0:T(8,128)S(1)}, u32[]{:S(2)}, u32[]{:S(2)}) %collective-permute-start.3) | collective-permute-done | bytes 114720 | tf_op jit(solution)/shard_map/ppermute | solution.py:330
  11.5 0.0 collective-permute-done.4.refs_5_
  11.5 0.0 collective-permute-done.refs_0_
  11.5 2.6 %collective-permute-start.5 = (f32[3,2,64,128]{3,2,1,0:T(8,128)S(1)}, f32[3,2,64,128]{3,2,1,0:T(8,128)S(1)}, u32[]{:S(2)}, u32[]{:S(2)}) collective-permute-start(f32[3,2,64,128]{3,2,1,0:T(8,128)S(1)} %shard_map.39), channel_id=1, source_target_pairs={{0,4},{1,5},{2,6},{3,7},{4,8},{5,9},{6,10},{7,11},{8,12},{9,13},{1... | collective-permute-start | bytes 589832 | tf_op jit(solution)/shard_map/ppermute | solution.py:330
  14.1 1.8 %shard_map.40.second = f32[3,2,64,128]{3,2,1,0:T(8,128)S(1)} custom-call(s32[2,2,8]{2,1,0:T(2,128)S(1)} %get-tuple-element.15.table_ref, f32[64,8,128]{2,1,0:T(8,128)S(1)} %collective-permute-done.refs_0_, f32[28,8,128]{2,1,0:T(8,128)S(1)} %collective-permute-done.1.refs_1_, f32[28,8,128]{2,1,0:T(8,128)S(1)} %collective-permute-done.2.refs_2_, ...), custom_call_target="tpu_custom_call" | custom-call | flops 15728640 | bytes 1048576 | tf_op jit(solution)/shard_map/pallas_call | solution.py:392
  15.9 0.1 collective-permute-start.6
  16.0 1.8 %shard_map.41.third = f32[3,2,64,128]{3,2,1,0:T(8,128)S(1)} custom-call(s32[2,2,8]{2,1,0:T(2,128)S(1)} %get-tuple-element.15.table_ref, f32[64,8,128]{2,1,0:T(8,128)S(1)} %collective-permute-done.refs_0_, f32[28,8,128]{2,1,0:T(8,128)S(1)} %collective-permute-done.1.refs_1_, f32[28,8,128]{2,1,0:T(8,128)S(1)} %collective-permute-done.2.refs_2_, ...), custom_call_target="tpu_custom_call" | custom-call | flops 15728640 | bytes 1048576 | tf_op jit(solution)/shard_map/pallas_call | solution.py:394
  17.8 0.7 %collective-permute-done.5.far = f32[3,2,64,128]{3,2,1,0:T(8,128)S(1)} collective-permute-done((f32[3,2,64,128]{3,2,1,0:T(8,128)S(1)}, f32[3,2,64,128]{3,2,1,0:T(8,128)S(1)}, u32[]{:S(2)}, u32[]{:S(2)}) %collective-permute-start.5) | collective-permute-done | bytes 196640 | tf_op jit(solution)/shard_map/ppermute | solution.py:330
  18.5 0.0 collective-permute-done.6.near
  18.5 0.9 %shard_map.42 = f32[3,2,2,64,128]{4,3,2,1,0:T(8,128)} custom-call(s32[2,2,8]{2,1,0:T(2,128)S(1)} %get-tuple-element.15.table_ref, f32[3,2,64,128]{3,2,1,0:T(8,128)S(1)} %collective-permute-done.5.far, f32[3,2,64,128]{3,2,1,0:T(8,128)S(1)} %shard_map.40.second, f32[3,2,64,128]{3,2,1,0:T(8,128)S(1)} %collective-permute-done.6.near, ...), custom_call_target="tpu_custom_call" | custom-call | bytes 1048576 | tf_op jit(solution)/shard_map/pallas_call | solution.py:397
  (1 shorter events, 0.0 us)
Async XLA Ops:
  1.1 10.4 %collective-permute-start = (f32[64,8,128]{2,1,0:T(8,128)S(1)}, f32[64,8,128]{2,1,0:T(8,128)S(1)}, u32[]{:S(2)}, u32[]{:S(2)}) collective-permute-start(f32[64,8,128]{2,1,0:T(8,128)S(1)} %get-tuple-element.16), channel_id=1, source_target_pairs={{0,4},{1,5},{2,6},{3,7},{4,8},{5,9},{6,10},{7,11},{8,12},{9,13},{1... | collective-permute-start | bytes 786440 | tf_op jit(solution)/shard_map/ppermute | solution.py:330
  2.0 8.3 %collective-permute-start.1 = (f32[28,8,128]{2,1,0:T(8,128)S(1)}, f32[28,8,128]{2,1,0:T(8,128)S(1)}, u32[]{:S(2)}, u32[]{:S(2)}) collective-permute-start(f32[28,8,128]{2,1,0:T(8,128)S(1)} %get-tuple-element.19), channel_id=1, source_target_pairs={{0,5},{1,4},{2,7},{3,6},{4,9},{5,8},{6,11},{7,10},{8,13},{9,12},{1... | collective-permute-start | bytes 344072 | tf_op jit(solution)/shard_map/ppermute | solution.py:330
  5.8 5.4 %collective-permute-start.2 = (f32[28,8,128]{2,1,0:T(8,128)S(1)}, f32[28,8,128]{2,1,0:T(8,128)S(1)}, u32[]{:S(2)}, u32[]{:S(2)}) collective-permute-start(f32[28,8,128]{2,1,0:T(8,128)S(1)} %get-tuple-element.20), channel_id=1, source_target_pairs={{0,4},{1,6},{2,5},{3,7},{4,8},{5,10},{6,9},{7,11},{8,12},{9,14},{1... | collective-permute-start | bytes 344072 | tf_op jit(solution)/shard_map/ppermute | solution.py:330
  5.8 5.7 %collective-permute-start.3 = (f32[28,8,128]{2,1,0:T(8,128)S(1)}, f32[28,8,128]{2,1,0:T(8,128)S(1)}, u32[]{:S(2)}, u32[]{:S(2)}) collective-permute-start(f32[28,8,128]{2,1,0:T(8,128)S(1)} %get-tuple-element.22), channel_id=1, source_target_pairs={{0,1},{1,0},{2,3},{3,2},{4,5},{5,4},{6,7},{7,6},{8,9},{9,8},{10,11... | collective-permute-start | bytes 344072 | tf_op jit(solution)/shard_map/ppermute | solution.py:330
  8.4 3.1 %collective-permute-start.4 = (f32[28,8,128]{2,1,0:T(8,128)S(1)}, f32[28,8,128]{2,1,0:T(8,128)S(1)}, u32[]{:S(2)}, u32[]{:S(2)}) collective-permute-start(f32[28,8,128]{2,1,0:T(8,128)S(1)} %get-tuple-element.23), channel_id=1, source_target_pairs={{0,4},{1,2},{2,1},{3,7},{4,0},{5,6},{6,5},{7,3},{8,12},{9,10},{10,... | collective-permute-start | bytes 344072 | tf_op jit(solution)/shard_map/ppermute | solution.py:330
  11.5 7.0 %collective-permute-start.5 = (f32[3,2,64,128]{3,2,1,0:T(8,128)S(1)}, f32[3,2,64,128]{3,2,1,0:T(8,128)S(1)}, u32[]{:S(2)}, u32[]{:S(2)}) collective-permute-start(f32[3,2,64,128]{3,2,1,0:T(8,128)S(1)} %shard_map.39), channel_id=1, source_target_pairs={{0,4},{1,5},{2,6},{3,7},{4,8},{5,9},{6,10},{7,11},{8,12},{9,13},{1... | collective-permute-start | bytes 589832 | tf_op jit(solution)/shard_map/ppermute | solution.py:330
  15.9 2.6 %collective-permute-start.6 = (f32[3,2,64,128]{3,2,1,0:T(8,128)S(1)}, f32[3,2,64,128]{3,2,1,0:T(8,128)S(1)}, u32[]{:S(2)}, u32[]{:S(2)}) collective-permute-start(f32[3,2,64,128]{3,2,1,0:T(8,128)S(1)} %shard_map.40.second), channel_id=1, source_target_pairs={{0,4},{1,5},{2,6},{3,7},{4,0},{5,1},{6,2},{7,3},{8,12},{9,13},{10,... | collective-permute-start | bytes 589832 | tf_op jit(solution)/shard_map/ppermute | solution.py:330

commit v3 on v2

--- a/solution.py
+++ b/solution.py
@@ -88,16 +88,20 @@
     return noise_ref[cycle, slot, tile, pl.ds(row, blocks, stride=TILE), :]
 
 
-def edges(state_ref, noise_ref, table_ref, xa, xb, ka, kb, kmain, later, *, islands):
+def edges(state_ref, noise_ref, table_ref, xa, xb, ka, kb, kmain, later, plan, *, islands):
     slots, tiles = state_ref.shape[1], state_ref.shape[2]
     rows = tiles * TILE
     island = lax.axis_index("dom")
     odd = lax.rem(lax.axis_index("lat"), 2)
     table = table_ref[...]
     _, wanted, _ = entries(table, 0, lax.rem(island + 1, islands))
-    kept, _, _ = entries(table, 0, island)
+    kept, _, foreign = entries(table, 0, island)
     sent = jnp.clip(wanted - slots, 0, slots - 1)
     kept = jnp.clip(kept, 0, slots - 1)
+    _, taken_slot, _ = entries(table, 1, lax.rem(island + 1, islands))
+    kept_slot, _, position = entries(table, 1, island)
+    for index, value in enumerate((taken_slot - slots == foreign, kept_slot == foreign, position == 1)):
+        plan[index] = jnp.full(plan.shape[1:], value.astype(jnp.float32))
     for slot, edge, bottom in ((sent, xa, 1 - odd), (sent, xb, odd), (kept, ka, 1 - odd), (kept, kb, odd)):
         tile = bottom * (tiles - 1)
         for field in range(3):
@@ -110,9 +114,9 @@
             kmain[field * rows + row] = state_row(state_ref, field, kept, row // TILE, row % TILE)
     for row in range(rows):
         kmain[3 * rows + row] = noise_row(noise_ref, 0, kept, row // TILE, row % TILE)
-    for slot in range(slots):
+    for index, slot in enumerate((1 - foreign, foreign)):
         for row in range(rows):
-            later[slot * rows + row] = noise_row(noise_ref, 1, slot, row // TILE, row % TILE)
+            later[index * rows + row] = noise_row(noise_ref, 1, slot, row // TILE, row % TILE)
 
 
 def tendency_rows(load, store, first, last, coriolis):
@@ -161,41 +165,33 @@
         below, here = here, above
 
 
-def forecast(slot, table, sources, out, state, middle, noise, bands):
+def forecast(arrived, sources, out, state, middle, noise, bands):
     main, xa, xb, kmain, ka, kb, later = sources
     rows = main.shape[0] // 4
     blocks = main.shape[1]
     wide = rows + 2 * HALO
-    island, band = lax.axis_index("dom"), lax.axis_index("lat")
+    band = lax.axis_index("lat")
     odd = lax.rem(band, 2)
-    _, _, foreign = entries(table, 0, island)
-    slot = jnp.clip(slot, 0, 1)
-    arrived = slot == foreign
+    arrived = arrived > 0.5
     inside_low = (band > 0).astype(jnp.float32)
     inside_high = (band < bands - 1).astype(jnp.float32)
 
-    def gather(whole, first, second):
+    for field in range(3):
+        for row in range(rows):
+            place = field * rows + row
+            state[field * wide + HALO + row] = jnp.where(arrived, main[place], kmain[place])
+    for row in range(rows):
+        noise[NEAR + row] = jnp.where(arrived, main[3 * rows + row], kmain[3 * rows + row])
+    for first, second, high in ((xa, ka, 1 - odd), (xb, kb, odd)):
+        inside = jnp.where(high == 1, inside_high, inside_low)
+        start, start_noise = high * (rows + HALO), high * (rows + NEAR)
         for field in range(3):
-            for row in range(rows):
-                state[field * wide + HALO + row] = whole[field * rows + row]
-        for row in range(rows):
-            noise[NEAR + row] = whole[3 * rows + row]
-        for edge, high in ((first, 1 - odd), (second, odd)):
-            inside = jnp.where(high == 1, inside_high, inside_low)
-            start, start_noise = high * (rows + HALO), high * (rows + NEAR)
-            for field in range(3):
-                for row in range(HALO):
-                    state[field * wide + start + row] = edge[field * HALO + row] * inside
-            for row in range(NEAR):
-                noise[start_noise + row] = edge[3 * HALO + row] * inside
-
-    @pl.when(arrived)
-    def _():
-        gather(main, xa, xb)
-
-    @pl.when(jnp.logical_not(arrived))
-    def _():
-        gather(kmain, ka, kb)
+            for row in range(HALO):
+                place = field * HALO + row
+                state[field * wide + start + row] = jnp.where(arrived, first[place], second[place]) * inside
+        for row in range(NEAR):
+            place = 3 * HALO + row
+            noise[start_noise + row] = jnp.where(arrived, first[place], second[place]) * inside
 
     def within(row, value):
         if row < HALO:
@@ -228,7 +224,8 @@
                         if cycle == 0:
                             value = value + noise[row - HALO + NEAR]
                         else:
-                            value = value + later[slot * rows + row - HALO]
+                            own = row - HALO
+                            value = value + jnp.where(arrived, later[rows + own], later[own])
                     if final:
                         own = row - HALO
                         value = value if field == 0 else value * (1.0 / half)
@@ -242,52 +239,38 @@
             tendency_rows(lambda field, row: middle[field * wide + row], to_state, margin, wide - margin, coriolis)
 
 
-def wanted_slot(table, islands):
-    _, slot, _ = entries(table, 1, lax.rem(lax.axis_index("dom") + 1, islands))
-    return slot - 2
-
-
-def kept_slot(table):
-    slot, _, _ = entries(table, 1, lax.axis_index("dom"))
-    return slot
-
-
 def odd_island():
     return lax.rem(lax.axis_index("dom"), 2)
 
 
-def payload_odd(table_ref, *refs, islands, bands):
+def payload_odd(plan, *refs, bands):
     *sources, out, state, middle, noise = refs
 
     @pl.when(odd_island() == 1)
     def _():
-        table = table_ref[...]
-        forecast(wanted_slot(table, islands), table, sources, out, state, middle, noise, bands)
-
-
-def payload_even(table_ref, *refs, islands, bands):
+        forecast(plan[0], sources, out, state, middle, noise, bands)
+
+
+def payload_even(plan, *refs, bands):
     *sources, out, state, middle, noise = refs
-    table = table_ref[...]
-    slot = jnp.where(odd_island() == 1, kept_slot(table), wanted_slot(table, islands))
-    forecast(slot, table, sources, out, state, middle, noise, bands)
-
-
-def keep_local(table_ref, *refs, bands):
+    forecast(plan[odd_island()], sources, out, state, middle, noise, bands)
+
+
+def keep_local(plan, *refs, bands):
     *sources, out, state, middle, noise = refs
 
     @pl.when(odd_island() == 0)
     def _():
-        table = table_ref[...]
-        forecast(kept_slot(table), table, sources, out, state, middle, noise, bands)
-
-
-def finish(table_ref, far, second, near, third, out, done):
-    _, _, foreign = entries(table_ref[...], 1, lax.axis_index("dom"))
+        forecast(plan[1], sources, out, state, middle, noise, bands)
+
+
+def finish(plan, far, second, near, third, out, done):
+    position = jnp.where(plan[2][0, 0] > 0.5, 1, 0)
 
     def write(kept, taken):
         copies = [
-            pltpu.make_async_copy(kept, out.at[:, 1 - foreign], done.at[0]),
-            pltpu.make_async_copy(taken, out.at[:, foreign], done.at[1]),
+            pltpu.make_async_copy(kept, out.at[:, 1 - position], done.at[0]),
+            pltpu.make_async_copy(taken, out.at[:, position], done.at[1]),
         ]
         for copy in copies:
             copy.start()
@@ -370,8 +353,10 @@
         [full, (VMEM, state_tiles.shape, real), (VMEM, noise_tiles.shape, real), (VMEM, table.shape, jnp.int32)],
         [pltpu.SemaphoreType.DMA((4,))],
     )(*(pltpu.with_memory_space_constraint(value, pltpu.HBM) for value in (state_tiles, noise_tiles, table)))
-    sends["xa"], sends["xb"], sends["ka"], sends["kb"], kmain, later = on_chip(
-        functools.partial(edges, islands=islands), [VMEM] * 3, [edge] * 4 + [full, later_rows]
+    sends["xa"], sends["xb"], sends["ka"], sends["kb"], kmain, later, plan = on_chip(
+        functools.partial(edges, islands=islands),
+        [VMEM] * 3,
+        [edge] * 4 + [full, later_rows, (VMEM, (3, blocks, LANES), real)],
     )(state_tiles, noise_tiles, table)
     places = {
         "main": following,
@@ -381,12 +366,12 @@
         "kb": across(1, 0),
     }
     got = {name: send(sends[name], places[name]) for name in ORDER}
-    sources = (table, got["main"], got["xa"], got["xb"], kmain, got["ka"], got["kb"], later)
+    sources = (plan, got["main"], got["xa"], got["xb"], kmain, got["ka"], got["kb"], later)
 
     work = [pltpu.VMEM((3 * wide, blocks, LANES), real)] * 2 + [pltpu.VMEM((rows + 2 * NEAR, blocks, LANES), real)]
     result = (3,) + state_tiles.shape[2:]
     flops = 60 * wide * columns * 4 * STEPS
-    sizes = dict(islands=islands, bands=bands)
+    sizes = dict(bands=bands)
     (first,) = on_chip(functools.partial(payload_odd, **sizes), [VMEM] * 8, [(VMEM, result, real)], work, flops)(*sources)
     far = send(first, following)
     (second,) = on_chip(functools.partial(payload_even, **sizes), [VMEM] * 8, [(VMEM, result, real)], work, flops)(*sources)
@@ -396,7 +381,7 @@
     )
     (out,) = on_chip(
         finish, [VMEM] * 5, [(HBM, state_tiles.shape, real)], [pltpu.SemaphoreType.DMA((2,))]
-    )(table, far, second, near, third)
+    )(plan, far, second, near, third)
     return from_row_tiles(out)
 
 

time: 19.5 us -> 19.4 us (level)
  Pallas kernels: 5.94 us -> 5.67 us
  transfers between devices with their start and end apart: 7 -> 7, of which waited for: 4 -> 4; matrix products, arithmetic and copies ran while one was open for 0% -> 0% of each run, Pallas kernels for 20% -> 19%
where the time goes in v3:
time: 19.4 us; the launch traced here: 19.2 us
  starting transfers between devices  10.8 us (56%)
  Pallas kernels  5.67 us (29%)
  waiting for transfers between devices  2.69 us (14%)
    ppermute x7, starting transfers between devices, send(): return lax.ppermute(value, ('dom', 'lat'), pairs)  10.8 us
    ppermute x7, waiting for transfers between devices, send(): return lax.ppermute(value, ('dom', 'lat'), pairs)  2.69 us
    pallas_call x1, Pallas kernels, body(): on_chip(functools.partial(keep_local, bands=bands), [VMEM] * 8, [(VMEM, r...  1.72 us
    pallas_call x1, Pallas kernels, body(): on_chip(functools.partial(payload_even, **sizes), [VMEM] * 8, [(VMEM, res...  1.71 us
    pallas_call x1, Pallas kernels, body(): on_chip(functools.partial(collect, islands=islands), [HBM] * 3, [full, (V...  1.13 us
    pallas_call x1, Pallas kernels, body(): on_chip(finish, [VMEM] * 5, [(HBM, state_tiles.shape, real)], [pltpu.Sema...  0.8 us
  transfers between devices with their start and end apart: 7, of which 4 were waited for; matrix products, arithmetic and copies ran while one was open for 0% of the time, Pallas kernels for 19%

profile of v3, /device:TPU:0, one launch (start us, length us, event | category | flops | bytes accessed | tf_op | source)
XLA Modules:
  0.0 19.2 jit_solution(8206916646808484878)
XLA Ops:
  0.0 1.1 %shard_map.37 = (f32[64,8,128]{2,1,0:T(8,128)S(1)}, f32[3,2,2,64,128]{4,3,2,1,0:T(8,128)S(1)}, f32[2,2,2,64,128]{4,3,2,1,0:T(8,128)S(1)}, s32[2,2,8]{2,1,0:T(2,128)S(1)}) custom-call(f32[3,2,2,64,128]{4,3,2,1,0:T(8,128)} %bitcast.16, f32[2,2,2,64,128]{4,3,2,1,0:T(8,128)} %bitcast.17, s32[2,2,8]{2,1,0:T(2,128)} %bitcast.18), custom_call_target="tpu_custom_call" | custom-call | bytes 1048576 | tf_op jit(solution)/shard_map/pallas_call | solution.py:350
  1.1 0.5 %collective-permute-start = (f32[64,8,128]{2,1,0:T(8,128)S(1)}, f32[64,8,128]{2,1,0:T(8,128)S(1)}, u32[]{:S(2)}, u32[]{:S(2)}) collective-permute-start(f32[64,8,128]{2,1,0:T(8,128)S(1)} %get-tuple-element.20), channel_id=1, source_target_pairs={{0,4},{1,5},{2,6},{3,7},{4,8},{5,9},{6,10},{7,11},{8,12},{9,13},{1... | collective-permute-start | bytes 786440 | tf_op jit(solution)/shard_map/ppermute | solution.py:313
  1.6 0.3 %shard_map.38 = (f32[28,8,128]{2,1,0:T(8,128)S(1)}, f32[28,8,128]{2,1,0:T(8,128)S(1)}, f32[28,8,128]{2,1,0:T(8,128)S(1)}, f32[28,8,128]{2,1,0:T(8,128)S(1)}, f32...) custom-call(f32[3,2,2,64,128]{4,3,2,1,0:T(8,128)S(1)} %get-tuple-element.16.state_ref, ...), custom_call_target="tpu_custom_call" | custom-call | bytes 1048576 | tf_op jit(solution)/shard_map/pallas_call | solution.py:356
  2.0 3.8 %collective-permute-start.1 = (f32[28,8,128]{2,1,0:T(8,128)S(1)}, f32[28,8,128]{2,1,0:T(8,128)S(1)}, u32[]{:S(2)}, u32[]{:S(2)}) collective-permute-start(f32[28,8,128]{2,1,0:T(8,128)S(1)} %get-tuple-element.21), channel_id=1, source_target_pairs={{0,5},{1,4},{2,7},{3,6},{4,9},{5,8},{6,11},{7,10},{8,13},{9,12},{1... | collective-permute-start | bytes 344072 | tf_op jit(solution)/shard_map/ppermute | solution.py:313
  5.8 0.0 collective-permute-start.2
  5.8 2.6 %collective-permute-start.3 = (f32[28,8,128]{2,1,0:T(8,128)S(1)}, f32[28,8,128]{2,1,0:T(8,128)S(1)}, u32[]{:S(2)}, u32[]{:S(2)}) collective-permute-start(f32[28,8,128]{2,1,0:T(8,128)S(1)} %get-tuple-element.24), channel_id=1, source_target_pairs={{0,1},{1,0},{2,3},{3,2},{4,5},{5,4},{6,7},{7,6},{8,9},{9,8},{10,11... | collective-permute-start | bytes 344072 | tf_op jit(solution)/shard_map/ppermute | solution.py:313
  8.4 1.3 %collective-permute-start.4 = (f32[28,8,128]{2,1,0:T(8,128)S(1)}, f32[28,8,128]{2,1,0:T(8,128)S(1)}, u32[]{:S(2)}, u32[]{:S(2)}) collective-permute-start(f32[28,8,128]{2,1,0:T(8,128)S(1)} %get-tuple-element.25), channel_id=1, source_target_pairs={{0,4},{1,2},{2,1},{3,7},{4,0},{5,6},{6,5},{7,3},{8,12},{9,10},{10,... | collective-permute-start | bytes 344072 | tf_op jit(solution)/shard_map/ppermute | solution.py:313
  9.7 0.5 %collective-permute-done.1.refs_1_ = f32[28,8,128]{2,1,0:T(8,128)S(1)} collective-permute-done((f32[28,8,128]{2,1,0:T(8,128)S(1)}, f32[28,8,128]{2,1,0:T(8,128)S(1)}, u32[]{:S(2)}, u32[]{:S(2)}) %collective-permute-start.1) | collective-permute-done | bytes 114720 | tf_op jit(solution)/shard_map/ppermute | solution.py:313
  10.2 0.9 %collective-permute-done.2.refs_2_ = f32[28,8,128]{2,1,0:T(8,128)S(1)} collective-permute-done((f32[28,8,128]{2,1,0:T(8,128)S(1)}, f32[28,8,128]{2,1,0:T(8,128)S(1)}, u32[]{:S(2)}, u32[]{:S(2)}) %collective-permute-start.2) | collective-permute-done | bytes 114720 | tf_op jit(solution)/shard_map/ppermute | solution.py:313
  11.2 0.3 %collective-permute-done.3.refs_4_ = f32[28,8,128]{2,1,0:T(8,128)S(1)} collective-permute-done((f32[28,8,128]{2,1,0:T(8,128)S(1)}, f32[28,8,128]{2,1,0:T(8,128)S(1)}, u32[]{:S(2)}, u32[]{:S(2)}) %collective-permute-start.3) | collective-permute-done | bytes 114720 | tf_op jit(solution)/shard_map/ppermute | solution.py:313
  11.5 0.0 collective-permute-done.4.refs_5_
  11.5 0.0 collective-permute-done.refs_0_
  11.5 2.5 %collective-permute-start.5 = (f32[3,2,64,128]{3,2,1,0:T(8,128)S(1)}, f32[3,2,64,128]{3,2,1,0:T(8,128)S(1)}, u32[]{:S(2)}, u32[]{:S(2)}) collective-permute-start(f32[3,2,64,128]{3,2,1,0:T(8,128)S(1)} %shard_map.39), channel_id=1, source_target_pairs={{0,4},{1,5},{2,6},{3,7},{4,8},{5,9},{6,10},{7,11},{8,12},{9,13},{1... | collective-permute-start | bytes 589832 | tf_op jit(solution)/shard_map/ppermute | solution.py:313
  14.0 1.7 %shard_map.40.second = f32[3,2,64,128]{3,2,1,0:T(8,128)S(1)} custom-call(f32[3,8,128]{2,1,0:T(8,128)S(1)} %get-tuple-element.19.plan, f32[64,8,128]{2,1,0:T(8,128)S(1)} %collective-permute-done.refs_0_, f32[28,8,128]{2,1,0:T(8,128)S(1)} %collective-permute-done.1.refs_1_, f32[28,8,128]{2,1,0:T(8,128)S(1)} %collective-permute-done.2.refs_2_, ...), custom_call_target="tpu_custom_call" | custom-call | flops 15728640 | bytes 1048576 | tf_op jit(solution)/shard_map/pallas_call | solution.py:377
  15.7 0.1 collective-permute-start.6
  15.8 1.7 %shard_map.41.third = f32[3,2,64,128]{3,2,1,0:T(8,128)S(1)} custom-call(f32[3,8,128]{2,1,0:T(8,128)S(1)} %get-tuple-element.19.plan, f32[64,8,128]{2,1,0:T(8,128)S(1)} %collective-permute-done.refs_0_, f32[28,8,128]{2,1,0:T(8,128)S(1)} %collective-permute-done.1.refs_1_, f32[28,8,128]{2,1,0:T(8,128)S(1)} %collective-permute-done.2.refs_2_, ...), custom_call_target="tpu_custom_call" | custom-call | flops 15728640 | bytes 1048576 | tf_op jit(solution)/shard_map/pallas_call | solution.py:379
  17.5 0.9 %collective-permute-done.5.far = f32[3,2,64,128]{3,2,1,0:T(8,128)S(1)} collective-permute-done((f32[3,2,64,128]{3,2,1,0:T(8,128)S(1)}, f32[3,2,64,128]{3,2,1,0:T(8,128)S(1)}, u32[]{:S(2)}, u32[]{:S(2)}) %collective-permute-start.5) | collective-permute-done | bytes 196640 | tf_op jit(solution)/shard_map/ppermute | solution.py:313
  18.4 0.0 collective-permute-done.6.near
  18.4 0.8 %shard_map.42 = f32[3,2,2,64,128]{4,3,2,1,0:T(8,128)} custom-call(f32[3,8,128]{2,1,0:T(8,128)S(1)} %get-tuple-element.19.plan, f32[3,2,64,128]{3,2,1,0:T(8,128)S(1)} %collective-permute-done.5.far, f32[3,2,64,128]{3,2,1,0:T(8,128)S(1)} %shard_map.40.second, f32[3,2,64,128]{3,2,1,0:T(8,128)S(1)} %collective-permute-done.6.near, ...), custom_call_target="tpu_custom_call" | custom-call | bytes 1048576 | tf_op jit(solution)/shard_map/pallas_call | solution.py:382
  (1 shorter events, 0.0 us)
Async XLA Ops:
  1.1 10.4 %collective-permute-start = (f32[64,8,128]{2,1,0:T(8,128)S(1)}, f32[64,8,128]{2,1,0:T(8,128)S(1)}, u32[]{:S(2)}, u32[]{:S(2)}) collective-permute-start(f32[64,8,128]{2,1,0:T(8,128)S(1)} %get-tuple-element.20), channel_id=1, source_target_pairs={{0,4},{1,5},{2,6},{3,7},{4,8},{5,9},{6,10},{7,11},{8,12},{9,13},{1... | collective-permute-start | bytes 786440 | tf_op jit(solution)/shard_map/ppermute | solution.py:313
  2.0 8.3 %collective-permute-start.1 = (f32[28,8,128]{2,1,0:T(8,128)S(1)}, f32[28,8,128]{2,1,0:T(8,128)S(1)}, u32[]{:S(2)}, u32[]{:S(2)}) collective-permute-start(f32[28,8,128]{2,1,0:T(8,128)S(1)} %get-tuple-element.21), channel_id=1, source_target_pairs={{0,5},{1,4},{2,7},{3,6},{4,9},{5,8},{6,11},{7,10},{8,13},{9,12},{1... | collective-permute-start | bytes 344072 | tf_op jit(solution)/shard_map/ppermute | solution.py:313
  5.8 5.4 %collective-permute-start.2 = (f32[28,8,128]{2,1,0:T(8,128)S(1)}, f32[28,8,128]{2,1,0:T(8,128)S(1)}, u32[]{:S(2)}, u32[]{:S(2)}) collective-permute-start(f32[28,8,128]{2,1,0:T(8,128)S(1)} %get-tuple-element.22), channel_id=1, source_target_pairs={{0,4},{1,6},{2,5},{3,7},{4,8},{5,10},{6,9},{7,11},{8,12},{9,14},{1... | collective-permute-start | bytes 344072 | tf_op jit(solution)/shard_map/ppermute | solution.py:313
  5.8 5.7 %collective-permute-start.3 = (f32[28,8,128]{2,1,0:T(8,128)S(1)}, f32[28,8,128]{2,1,0:T(8,128)S(1)}, u32[]{:S(2)}, u32[]{:S(2)}) collective-permute-start(f32[28,8,128]{2,1,0:T(8,128)S(1)} %get-tuple-element.24), channel_id=1, source_target_pairs={{0,1},{1,0},{2,3},{3,2},{4,5},{5,4},{6,7},{7,6},{8,9},{9,8},{10,11... | collective-permute-start | bytes 344072 | tf_op jit(solution)/shard_map/ppermute | solution.py:313
  8.4 3.1 %collective-permute-start.4 = (f32[28,8,128]{2,1,0:T(8,128)S(1)}, f32[28,8,128]{2,1,0:T(8,128)S(1)}, u32[]{:S(2)}, u32[]{:S(2)}) collective-permute-start(f32[28,8,128]{2,1,0:T(8,128)S(1)} %get-tuple-element.25), channel_id=1, source_target_pairs={{0,4},{1,2},{2,1},{3,7},{4,0},{5,6},{6,5},{7,3},{8,12},{9,10},{10,... | collective-permute-start | bytes 344072 | tf_op jit(solution)/shard_map/ppermute | solution.py:313
  11.5 6.9 %collective-permute-start.5 = (f32[3,2,64,128]{3,2,1,0:T(8,128)S(1)}, f32[3,2,64,128]{3,2,1,0:T(8,128)S(1)}, u32[]{:S(2)}, u32[]{:S(2)}) collective-permute-start(f32[3,2,64,128]{3,2,1,0:T(8,128)S(1)} %shard_map.39), channel_id=1, source_target_pairs={{0,4},{1,5},{2,6},{3,7},{4,8},{5,9},{6,10},{7,11},{8,12},{9,13},{1... | collective-permute-start | bytes 589832 | tf_op jit(solution)/shard_map/ppermute | solution.py:313
  15.7 2.7 %collective-permute-start.6 = (f32[3,2,64,128]{3,2,1,0:T(8,128)S(1)}, f32[3,2,64,128]{3,2,1,0:T(8,128)S(1)}, u32[]{:S(2)}, u32[]{:S(2)}) collective-permute-start(f32[3,2,64,128]{3,2,1,0:T(8,128)S(1)} %shard_map.40.second), channel_id=1, source_target_pairs={{0,4},{1,5},{2,6},{3,7},{4,0},{5,1},{6,2},{7,3},{8,12},{9,13},{10,... | collective-permute-start | bytes 589832 | tf_op jit(solution)/shard_map/ppermute | solution.py:313

commit v4 on v3

--- a/solution.py
+++ b/solution.py
@@ -243,21 +243,135 @@
     return lax.rem(lax.axis_index("dom"), 2)
 
 
-def payload_odd(plan, *refs, bands):
-    *sources, out, state, middle, noise = refs
-
+def each_stage():
+    for cycle in range(FILTER_ROUNDS):
+        for step in range(STEPS):
+            stage = 2 * (cycle * STEPS + step) + 1
+            yield stage, False, False
+            yield stage + 1, True, step == STEPS - 1
+
+
+def coriolis_of(rows, bands):
+    start = (lax.axis_index("lat") * rows - HALO).astype(jnp.float32)
+    slope = time_step * rotation * 2.0 / (rows * bands)
+    base = slope * (start + 0.5) - time_step * rotation
+    return lambda row: base + slope * row
+
+
+def inner(plan, main, kmain, xa, xb, out, *, bands):
     @pl.when(odd_island() == 1)
     def _():
-        forecast(plan[0], sources, out, state, middle, noise, bands)
+        rows = kmain.shape[0] // 4
+        coriolis = coriolis_of(rows, bands)
+        arrived = plan[0] > 0.5
+
+        def place(stage, field, row):
+            return (stage * 3 + field) * rows + row - HALO
+
+        noise = 3 * HALO * rows
+        for row in range(3 * rows):
+            out[row] = jnp.where(arrived, main[row], kmain[row])
+        for row in range(rows):
+            out[noise + row] = jnp.where(arrived, main[3 * rows + row], kmain[3 * rows + row])
+        for stage, ends_step, ends_cycle in each_stage():
+            if stage == HALO:
+                break
+
+            def store(row, *values, stage=stage, ends_step=ends_step, ends_cycle=ends_cycle):
+                for field, value in enumerate(values):
+                    if ends_step:
+                        value = 0.5 * (out[place(stage - 2, field, row)] + value)
+                    if ends_cycle and field == 0:
+                        value = value + out[noise + row - HALO]
+                    out[place(stage, field, row)] = value
+
+            def load(field, row, stage=stage):
+                return out[place(stage - 1, field, row)]
+
+            tendency_rows(load, store, HALO + stage, HALO + rows - stage, coriolis)
+
+
+def outer(plan, inside, xa, xb, ka, kb, later, out, work, noise, *, bands):
+    @pl.when(odd_island() == 1)
+    def _():
+        rows = out.shape[1] * TILE
+        blocks = inside.shape[1]
+        band = lax.axis_index("lat")
+        odd = lax.rem(band, 2)
+        arrived = plan[0] > 0.5
+        coriolis = coriolis_of(rows, bands)
+        inner_side = ((band > 0).astype(jnp.float32), (band < bands - 1).astype(jnp.float32))
+        size = 3 * HALO * HALO
+
+        for first, second, high in ((xa, ka, 1 - odd), (xb, kb, odd)):
+            keep_rows = jnp.where(high == 1, inner_side[1], inner_side[0])
+            for row in range(3 * HALO):
+                work[high * size + row] = jnp.where(arrived, first[row], second[row]) * keep_rows
+            for row in range(NEAR):
+                place = 3 * HALO + row
+                noise[high * NEAR + row] = jnp.where(arrived, first[place], second[place]) * keep_rows
+
+        def first_row(side, stage):
+            return HALO + rows - stage if side else stage
+
+        def outside(row):
+            return row < HALO or row >= HALO + rows
+
+        def load(side, stage, field, row):
+            local = row - first_row(side, stage)
+            if 0 <= local < HALO:
+                return work[side * size + (stage * 3 + field) * HALO + local]
+            return inside[(stage * 3 + field) * rows + row - HALO]
+
+        for stage, ends_step, ends_cycle in each_stage():
+            for side in range(2):
+
+                def store(row, *values, stage=stage, side=side, ends_step=ends_step, ends_cycle=ends_cycle):
+                    own = row - HALO
+                    for field, value in enumerate(values):
+                        if ends_step:
+                            value = 0.5 * (load(side, stage - 2, field, row) + value)
+                        if stage == HALO:
+                            if field == 0:
+                                value = value + jnp.where(arrived, later[rows + own], later[own])
+                            else:
+                                value = value * (1.0 / half)
+                            out[field, own // TILE, pl.ds(own % TILE, blocks, stride=TILE), :] = value
+                            continue
+                        if ends_cycle and field == 0:
+                            if outside(row):
+                                value = value + noise[side * NEAR + (own - rows if side else own + NEAR)]
+                            else:
+                                value = value + inside[3 * HALO * rows + own]
+                        if outside(row):
+                            value = value * inner_side[side]
+                        work[side * size + (stage * 3 + field) * HALO + row - first_row(side, stage)] = value
+
+                start = first_row(side, stage)
+                tendency_rows(
+                    lambda field, row, stage=stage, side=side: load(side, stage - 1, field, row),
+                    store,
+                    start,
+                    start + HALO,
+                    coriolis,
+                )
 
 
 def payload_even(plan, *refs, bands):
-    *sources, out, state, middle, noise = refs
-    forecast(plan[odd_island()], sources, out, state, middle, noise, bands)
+    main, xa, xb, kmain, ka, kb, kc, later, out, state, middle, noise = refs
+
+    @pl.when(odd_island() == 1)
+    def _():
+        forecast(plan[1], (main, xa, xb, kmain, ka, kb, later), out, state, middle, noise, bands)
+
+    @pl.when(odd_island() == 0)
+    def _():
+        forecast(plan[0], (main, xa, xb, kmain, ka, kc, later), out, state, middle, noise, bands)
 
 
 def keep_local(plan, *refs, bands):
-    *sources, out, state, middle, noise = refs
+    main, xa, xb, kmain, ka, _, kc, later, out, state, middle, noise = refs
+    sources = main, xa, xb, kmain, ka, kc, later
 
     @pl.when(odd_island() == 0)
     def _():
@@ -313,7 +427,7 @@
     return lax.ppermute(value, ("dom", "lat"), pairs)
 
 
-ORDER = ("main", "xa", "xb", "ka", "kb")
+ORDER = ("main", "xa", "xb", "ka", "kb", "kc")
 
 
 def body(states, stir_noise, ancestors):
@@ -340,6 +454,17 @@
             if partner is not None:
                 return (island + step) % islands, partner
             return ((island + step) % islands, band) if step else beside(island, band)
+
+        return place
+
+    def only(parity):
+        def place(island, band):
+            partner = pair(band, 1)
+            if partner is None:
+                return beside(island, band)
+            if island % 2 == parity:
+                return island, partner
+            return (island + 2) % islands, band
 
         return place
 
@@ -363,21 +488,33 @@
         "xa": across(0, 1),
         "xb": across(1, 1),
         "ka": across(0, 0),
-        "kb": across(1, 0),
+        "kb": only(1),
+        "kc": only(0),
     }
+    sends["kc"] = sends["kb"]
     got = {name: send(sends[name], places[name]) for name in ORDER}
-    sources = (plan, got["main"], got["xa"], got["xb"], kmain, got["ka"], got["kb"], later)
+    late_sources = (plan, got["main"], got["xa"], got["xb"], kmain, got["ka"], got["kb"], got["kc"], later)
 
     work = [pltpu.VMEM((3 * wide, blocks, LANES), real)] * 2 + [pltpu.VMEM((rows + 2 * NEAR, blocks, LANES), real)]
     result = (3,) + state_tiles.shape[2:]
     flops = 60 * wide * columns * 4 * STEPS
     sizes = dict(bands=bands)
-    (first,) = on_chip(functools.partial(payload_odd, **sizes), [VMEM] * 8, [(VMEM, result, real)], work, flops)(*sources)
+    (inside,) = on_chip(
+        functools.partial(inner, **sizes),
+        [VMEM] * 5,
+        [(VMEM, ((3 * HALO + 1) * rows, blocks, LANES), real)],
+    )(plan, got["main"], kmain, got["xa"], got["xb"])
+    (first,) = on_chip(
+        functools.partial(outer, **sizes),
+        [VMEM] * 7,
+        [(VMEM, result, real)],
+        [pltpu.VMEM((6 * HALO * HALO, blocks, LANES), real), pltpu.VMEM((2 * NEAR, blocks, LANES), real)],
+    )(plan, inside, got["xa"], got["xb"], got["ka"], got["kb"], later)
     far = send(first, following)
-    (second,) = on_chip(functools.partial(payload_even, **sizes), [VMEM] * 8, [(VMEM, result, real)], work, flops)(*sources)
+    (second,) = on_chip(functools.partial(payload_even, **sizes), [VMEM] * 9, [(VMEM, result, real)], work, flops)(*late_sources)
     near = send(second, beside)
-    (third,) = on_chip(functools.partial(keep_local, bands=bands), [VMEM] * 8, [(VMEM, result, real)], work, flops)(
-        *sources
+    (third,) = on_chip(functools.partial(keep_local, bands=bands), [VMEM] * 9, [(VMEM, result, real)], work, flops)(
+        *late_sources
     )
     (out,) = on_chip(
         finish, [VMEM] * 5, [(HBM, state_tiles.shape, real)], [pltpu.SemaphoreType.DMA((2,))]

time: 19.4 us -> 18.9 us (0.974)
  starting transfers between devices: 10.8 us -> 10.4 us
    ppermute x7 -> x8, starting transfers between devices: 10.8 us -> 10.4 us  [send(): return lax.ppermute(value, ('dom', 'lat'), pairs)]
    ppermute x7 -> x8, waiting for transfers between devices: 2.69 us -> 2.65 us  [send(): return lax.ppermute(value, ('dom', 'lat'), pairs)]
    pallas_call x3 -> x4, Pallas kernels: 3.43 us -> 3.44 us  [the longest x1 1.74 us: body(): on_chip(functools.partial(payload_even, **sizes), [VMEM] * 9, [(VMEM, res...]
  transfers between devices with their start and end apart: 7 -> 8, of which waited for: 4 -> 4; matrix products, arithmetic and copies ran while one was open for 0% -> 0% of each run, Pallas kernels for 19% -> 20%
where the time goes in v4:
time: 18.9 us; the launch traced here: 18.7 us
  starting transfers between devices  10.4 us (55%)
  Pallas kernels  5.68 us (30%)
  waiting for transfers between devices  2.65 us (14%)
    ppermute x8, starting transfers between devices, send(): return lax.ppermute(value, ('dom', 'lat'), pairs)  10.4 us
    ppermute x8, waiting for transfers between devices, send(): return lax.ppermute(value, ('dom', 'lat'), pairs)  2.65 us
    pallas_call x1, Pallas kernels, body(): on_chip(functools.partial(payload_even, **sizes), [VMEM] * 9, [(VMEM, res...  1.74 us
    pallas_call x1, Pallas kernels, body(): on_chip(functools.partial(keep_local, bands=bands), [VMEM] * 9, [(VMEM, r...  1.7 us
    pallas_call x1, Pallas kernels, body(): on_chip(functools.partial(collect, islands=islands), [HBM] * 3, [full, (V...  1.13 us
    pallas_call x1, Pallas kernels, body(): on_chip(finish, [VMEM] * 5, [(HBM, state_tiles.shape, real)], [pltpu.Sema...  0.8 us
  transfers between devices with their start and end apart: 8, of which 4 were waited for; matrix products, arithmetic and copies ran while one was open for 0% of the time, Pallas kernels for 20%

profile of v4, /device:TPU:0, one launch (start us, length us, event | category | flops | bytes accessed | tf_op | source)
XLA Modules:
  0.0 18.7 jit_solution(7211382761760438075)
XLA Ops:
  0.0 1.1 %shard_map.37 = (f32[64,8,128]{2,1,0:T(8,128)S(1)}, f32[3,2,2,64,128]{4,3,2,1,0:T(8,128)S(1)}, f32[2,2,2,64,128]{4,3,2,1,0:T(8,128)S(1)}, s32[2,2,8]{2,1,0:T(2,128)S(1)}) custom-call(f32[3,2,2,64,128]{4,3,2,1,0:T(8,128)} %bitcast.16, f32[2,2,2,64,128]{4,3,2,1,0:T(8,128)} %bitcast.17, s32[2,2,8]{2,1,0:T(2,128)} %bitcast.18), custom_call_target="tpu_custom_call" | custom-call | bytes 1048576 | tf_op jit(solution)/shard_map/pallas_call | solution.py:475
  1.1 0.5 %collective-permute-start = (f32[64,8,128]{2,1,0:T(8,128)S(1)}, f32[64,8,128]{2,1,0:T(8,128)S(1)}, u32[]{:S(2)}, u32[]{:S(2)}) collective-permute-start(f32[64,8,128]{2,1,0:T(8,128)S(1)} %get-tuple-element.20), channel_id=1, source_target_pairs={{0,4},{1,5},{2,6},{3,7},{4,8},{5,9},{6,10},{7,11},{8,12},{9,13},{1... | collective-permute-start | bytes 786440 | tf_op jit(solution)/shard_map/ppermute | solution.py:427
  1.6 0.3 %shard_map.38 = (f32[28,8,128]{2,1,0:T(8,128)S(1)}, f32[28,8,128]{2,1,0:T(8,128)S(1)}, f32[28,8,128]{2,1,0:T(8,128)S(1)}, f32[28,8,128]{2,1,0:T(8,128)S(1)}, f32...) custom-call(f32[3,2,2,64,128]{4,3,2,1,0:T(8,128)S(1)} %get-tuple-element.16.state_ref, ...), custom_call_target="tpu_custom_call" | custom-call | bytes 1048576 | tf_op jit(solution)/shard_map/pallas_call | solution.py:481
  2.0 3.8 %collective-permute-start.1 = (f32[28,8,128]{2,1,0:T(8,128)S(1)}, f32[28,8,128]{2,1,0:T(8,128)S(1)}, u32[]{:S(2)}, u32[]{:S(2)}) collective-permute-start(f32[28,8,128]{2,1,0:T(8,128)S(1)} %get-tuple-element.22), channel_id=1, source_target_pairs={{0,5},{1,4},{2,7},{3,6},{4,9},{5,8},{6,11},{7,10},{8,13},{9,12},{1... | collective-permute-start | bytes 344072 | tf_op jit(solution)/shard_map/ppermute | solution.py:427
  5.8 0.0 collective-permute-start.2
  5.8 2.6 %collective-permute-start.3 = (f32[28,8,128]{2,1,0:T(8,128)S(1)}, f32[28,8,128]{2,1,0:T(8,128)S(1)}, u32[]{:S(2)}, u32[]{:S(2)}) collective-permute-start(f32[28,8,128]{2,1,0:T(8,128)S(1)} %get-tuple-element.24), channel_id=1, source_target_pairs={{0,1},{1,0},{2,3},{3,2},{4,5},{5,4},{6,7},{7,6},{8,9},{9,8},{10,11... | collective-permute-start | bytes 344072 | tf_op jit(solution)/shard_map/ppermute | solution.py:427
  8.4 1.3 %collective-permute-start.4 = (f32[28,8,128]{2,1,0:T(8,128)S(1)}, f32[28,8,128]{2,1,0:T(8,128)S(1)}, u32[]{:S(2)}, u32[]{:S(2)}) collective-permute-start(f32[28,8,128]{2,1,0:T(8,128)S(1)} %get-tuple-element.25), channel_id=1, source_target_pairs={{0,4},{1,9},{2,10},{3,7},{4,0},{5,6},{6,5},{7,3},{8,12},{9,17},{10... | collective-permute-start | bytes 344072 | tf_op jit(solution)/shard_map/ppermute | solution.py:427
  9.7 0.5 %collective-permute-done.1.xa.refs_1_ = f32[28,8,128]{2,1,0:T(8,128)S(1)} collective-permute-done((f32[28,8,128]{2,1,0:T(8,128)S(1)}, f32[28,8,128]{2,1,0:T(8,128)S(1)}, u32[]{:S(2)}, u32[]{:S(2)}) %collective-permute-start.1) | collective-permute-done | bytes 114720 | tf_op jit(solution)/shard_map/ppermute | solution.py:427
  10.2 0.0 collective-permute-start.6
  10.2 0.9 %collective-permute-done.2.xb.refs_2_ = f32[28,8,128]{2,1,0:T(8,128)S(1)} collective-permute-done((f32[28,8,128]{2,1,0:T(8,128)S(1)}, f32[28,8,128]{2,1,0:T(8,128)S(1)}, u32[]{:S(2)}, u32[]{:S(2)}) %collective-permute-start.2) | collective-permute-done | bytes 114720 | tf_op jit(solution)/shard_map/ppermute | solution.py:427
  11.2 0.0 collective-permute-done.main.refs_0_
  11.2 0.3 %collective-permute-done.3.ka.refs_4_ = f32[28,8,128]{2,1,0:T(8,128)S(1)} collective-permute-done((f32[28,8,128]{2,1,0:T(8,128)S(1)}, f32[28,8,128]{2,1,0:T(8,128)S(1)}, u32[]{:S(2)}, u32[]{:S(2)}) %collective-permute-start.3) | collective-permute-done | bytes 114720 | tf_op jit(solution)/shard_map/ppermute | solution.py:427
  11.5 0.0 collective-permute-done.4.kb.refs_5_
  11.5 2.0 %collective-permute-start.5 = (f32[3,2,64,128]{3,2,1,0:T(8,128)S(1)}, f32[3,2,64,128]{3,2,1,0:T(8,128)S(1)}, u32[]{:S(2)}, u32[]{:S(2)}) collective-permute-start(f32[3,2,64,128]{3,2,1,0:T(8,128)S(1)} %shard_map.40), channel_id=1, source_target_pairs={{0,4},{1,5},{2,6},{3,7},{4,8},{5,9},{6,10},{7,11},{8,12},{9,13},{1... | collective-permute-start | bytes 589832 | tf_op jit(solution)/shard_map/ppermute | solution.py:427
  13.5 0.0 collective-permute-done.6.refs_6_
  13.6 1.7 %shard_map.41.second = f32[3,2,64,128]{3,2,1,0:T(8,128)S(1)} custom-call(f32[3,8,128]{2,1,0:T(8,128)S(1)} %get-tuple-element.19.plan, f32[64,8,128]{2,1,0:T(8,128)S(1)} %collective-permute-done.main.refs_0_, f32[28,8,128]{2,1,0:T(8,128)S(1)} %collective-permute-done.1.xa.refs_1_, f32[28,8,128]{2,1,0:T(8,128)S(1)} %collective-permute-done.2.xb.refs_2_, ...), custom_call_target="tpu_custom_call" | custom-call | flops 15728640 | bytes 1048576 | tf_op jit(solution)/shard_map/pallas_call | solution.py:514
  15.3 0.1 collective-permute-start.7
  15.4 1.7 %shard_map.42.third = f32[3,2,64,128]{3,2,1,0:T(8,128)S(1)} custom-call(f32[3,8,128]{2,1,0:T(8,128)S(1)} %get-tuple-element.19.plan, f32[64,8,128]{2,1,0:T(8,128)S(1)} %collective-permute-done.main.refs_0_, f32[28,8,128]{2,1,0:T(8,128)S(1)} %collective-permute-done.1.xa.refs_1_, f32[28,8,128]{2,1,0:T(8,128)S(1)} %collective-permute-done.2.xb.refs_2_, ...), custom_call_target="tpu_custom_call" | custom-call | flops 15728640 | bytes 1048576 | tf_op jit(solution)/shard_map/pallas_call | solution.py:516
  17.1 0.8 %collective-permute-done.5.far = f32[3,2,64,128]{3,2,1,0:T(8,128)S(1)} collective-permute-done((f32[3,2,64,128]{3,2,1,0:T(8,128)S(1)}, f32[3,2,64,128]{3,2,1,0:T(8,128)S(1)}, u32[]{:S(2)}, u32[]{:S(2)}) %collective-permute-start.5) | collective-permute-done | bytes 196640 | tf_op jit(solution)/shard_map/ppermute | solution.py:427
  17.9 0.0 collective-permute-done.7.near
  17.9 0.8 %shard_map.43 = f32[3,2,2,64,128]{4,3,2,1,0:T(8,128)} custom-call(f32[3,8,128]{2,1,0:T(8,128)S(1)} %get-tuple-element.19.plan, f32[3,2,64,128]{3,2,1,0:T(8,128)S(1)} %collective-permute-done.5.far, f32[3,2,64,128]{3,2,1,0:T(8,128)S(1)} %shard_map.41.second, f32[3,2,64,128]{3,2,1,0:T(8,128)S(1)} %collective-permute-done.7.near, ...), custom_call_target="tpu_custom_call" | custom-call | bytes 1048576 | tf_op jit(solution)/shard_map/pallas_call | solution.py:519
  (2 shorter events, 0.0 us)
Async XLA Ops:
  1.1 10.1 %collective-permute-start = (f32[64,8,128]{2,1,0:T(8,128)S(1)}, f32[64,8,128]{2,1,0:T(8,128)S(1)}, u32[]{:S(2)}, u32[]{:S(2)}) collective-permute-start(f32[64,8,128]{2,1,0:T(8,128)S(1)} %get-tuple-element.20), channel_id=1, source_target_pairs={{0,4},{1,5},{2,6},{3,7},{4,8},{5,9},{6,10},{7,11},{8,12},{9,13},{1... | collective-permute-start | bytes 786440 | tf_op jit(solution)/shard_map/ppermute | solution.py:427
  2.0 8.3 %collective-permute-start.1 = (f32[28,8,128]{2,1,0:T(8,128)S(1)}, f32[28,8,128]{2,1,0:T(8,128)S(1)}, u32[]{:S(2)}, u32[]{:S(2)}) collective-permute-start(f32[28,8,128]{2,1,0:T(8,128)S(1)} %get-tuple-element.22), channel_id=1, source_target_pairs={{0,5},{1,4},{2,7},{3,6},{4,9},{5,8},{6,11},{7,10},{8,13},{9,12},{1... | collective-permute-start | bytes 344072 | tf_op jit(solution)/shard_map/ppermute | solution.py:427
  5.8 5.4 %collective-permute-start.2 = (f32[28,8,128]{2,1,0:T(8,128)S(1)}, f32[28,8,128]{2,1,0:T(8,128)S(1)}, u32[]{:S(2)}, u32[]{:S(2)}) collective-permute-start(f32[28,8,128]{2,1,0:T(8,128)S(1)} %get-tuple-element.23), channel_id=1, source_target_pairs={{0,4},{1,6},{2,5},{3,7},{4,8},{5,10},{6,9},{7,11},{8,12},{9,14},{1... | collective-permute-start | bytes 344072 | tf_op jit(solution)/shard_map/ppermute | solution.py:427
  5.8 5.7 %collective-permute-start.3 = (f32[28,8,128]{2,1,0:T(8,128)S(1)}, f32[28,8,128]{2,1,0:T(8,128)S(1)}, u32[]{:S(2)}, u32[]{:S(2)}) collective-permute-start(f32[28,8,128]{2,1,0:T(8,128)S(1)} %get-tuple-element.24), channel_id=1, source_target_pairs={{0,1},{1,0},{2,3},{3,2},{4,5},{5,4},{6,7},{7,6},{8,9},{9,8},{10,11... | collective-permute-start | bytes 344072 | tf_op jit(solution)/shard_map/ppermute | solution.py:427
  8.4 3.1 %collective-permute-start.4 = (f32[28,8,128]{2,1,0:T(8,128)S(1)}, f32[28,8,128]{2,1,0:T(8,128)S(1)}, u32[]{:S(2)}, u32[]{:S(2)}) collective-permute-start(f32[28,8,128]{2,1,0:T(8,128)S(1)} %get-tuple-element.25), channel_id=1, source_target_pairs={{0,4},{1,9},{2,10},{3,7},{4,0},{5,6},{6,5},{7,3},{8,12},{9,17},{10... | collective-permute-start | bytes 344072 | tf_op jit(solution)/shard_map/ppermute | solution.py:427
  10.2 3.3 %collective-permute-start.6 = (f32[28,8,128]{2,1,0:T(8,128)S(1)}, f32[28,8,128]{2,1,0:T(8,128)S(1)}, u32[]{:S(2)}, u32[]{:S(2)}) collective-permute-start(f32[28,8,128]{2,1,0:T(8,128)S(1)} %get-tuple-element.25), channel_id=1, source_target_pairs={{0,4},{1,2},{2,1},{3,7},{4,0},{5,13},{6,14},{7,3},{8,12},{9,10},{1... | collective-permute-start | bytes 344072 | tf_op jit(solution)/shard_map/ppermute | solution.py:427
  11.5 6.4 %collective-permute-start.5 = (f32[3,2,64,128]{3,2,1,0:T(8,128)S(1)}, f32[3,2,64,128]{3,2,1,0:T(8,128)S(1)}, u32[]{:S(2)}, u32[]{:S(2)}) collective-permute-start(f32[3,2,64,128]{3,2,1,0:T(8,128)S(1)} %shard_map.40), channel_id=1, source_target_pairs={{0,4},{1,5},{2,6},{3,7},{4,8},{5,9},{6,10},{7,11},{8,12},{9,13},{1... | collective-permute-start | bytes 589832 | tf_op jit(solution)/shard_map/ppermute | solution.py:427
  15.3 2.7 %collective-permute-start.7 = (f32[3,2,64,128]{3,2,1,0:T(8,128)S(1)}, f32[3,2,64,128]{3,2,1,0:T(8,128)S(1)}, u32[]{:S(2)}, u32[]{:S(2)}) collective-permute-start(f32[3,2,64,128]{3,2,1,0:T(8,128)S(1)} %shard_map.41.second), channel_id=1, source_target_pairs={{0,4},{1,5},{2,6},{3,7},{4,0},{5,1},{6,2},{7,3},{8,12},{9,13},{10,... | collective-permute-start | bytes 589832 | tf_op jit(solution)/shard_map/ppermute | solution.py:427

commit v5 on v4

--- a/solution.py
+++ b/solution.py
@@ -120,6 +120,11 @@
 
 
 def tendency_rows(load, store, first, last, coriolis):
+    for _ in row_steps(load, store, first, last, coriolis):
+        pass
+
+
+def row_steps(load, store, first, last, coriolis):
     blocks = load(0, first).shape[0]
     lane = lax.broadcasted_iota(jnp.int32, (blocks, LANES), 1)
     at_end, at_start = lane == LANES - 1, lane == 0
@@ -163,6 +168,7 @@
         )
         store(row, h_new, u_new, v_new)
         below, here = here, above
+        yield row
 
 
 def forecast(arrived, sources, out, state, middle, noise, bands):
@@ -324,6 +330,7 @@
             return inside[(stage * 3 + field) * rows + row - HALO]
 
         for stage, ends_step, ends_cycle in each_stage():
+            steps = []
             for side in range(2):
 
                 def store(row, *values, stage=stage, side=side, ends_step=ends_step, ends_cycle=ends_cycle):
@@ -348,13 +355,17 @@
                         work[side * size + (stage * 3 + field) * HALO + row - first_row(side, stage)] = value
 
                 start = first_row(side, stage)
-                tendency_rows(
-                    lambda field, row, stage=stage, side=side: load(side, stage - 1, field, row),
-                    store,
-                    start,
-                    start + HALO,
-                    coriolis,
+                steps.append(
+                    row_steps(
+                        lambda field, row, stage=stage, side=side: load(side, stage - 1, field, row),
+                        store,
+                        start,
+                        start + HALO,
+                        coriolis,
+                    )
                 )
+            for _ in zip(*steps, strict=True):
+                pass
 
 
 def payload_even(plan, *refs, bands):
@@ -453,7 +464,7 @@
             partner = pair(band, turn)
             if partner is not None:
                 return (island + step) % islands, partner
-            return ((island + step) % islands, band) if step else beside(island, band)
+            return beside(island, band)
 
         return place
 

time: 18.9 us -> 18.9 us (level)
  transfers between devices with their start and end apart: 8 -> 8, of which waited for: 4 -> 3; matrix products, arithmetic and copies ran while one was open for 0% -> 0% of each run, Pallas kernels for 20% -> 20%
where the time goes in v5:
time: 18.9 us; the launch traced here: 18.7 us
  starting transfers between devices  10.3 us (54%)
  Pallas kernels  5.7 us (30%)
  waiting for transfers between devices  2.62 us (14%)
    ppermute x8, starting transfers between devices, send(): return lax.ppermute(value, ('dom', 'lat'), pairs)  10.3 us
    ppermute x8, waiting for transfers between devices, send(): return lax.ppermute(value, ('dom', 'lat'), pairs)  2.62 us
    pallas_call x1, Pallas kernels, body(): on_chip(functools.partial(payload_even, **sizes), [VMEM] * 9, [(VMEM, res...  1.74 us
    pallas_call x1, Pallas kernels, body(): on_chip(functools.partial(keep_local, bands=bands), [VMEM] * 9, [(VMEM, r...  1.7 us
    pallas_call x1, Pallas kernels, body(): on_chip(functools.partial(collect, islands=islands), [HBM] * 3, [full, (V...  1.13 us
    pallas_call x1, Pallas kernels, body(): on_chip(finish, [VMEM] * 5, [(HBM, state_tiles.shape, real)], [pltpu.Sema...  0.8 us
  transfers between devices with their start and end apart: 8, of which 3 were waited for; matrix products, arithmetic and copies ran while one was open for 0% of the time, Pallas kernels for 20%

profile of v5, /device:TPU:0, one launch (start us, length us, event | category | flops | bytes accessed | tf_op | source)
XLA Modules:
  0.0 18.7 jit_solution(16302769553947802729)
XLA Ops:
  0.0 1.1 %shard_map.37 = (f32[64,8,128]{2,1,0:T(8,128)S(1)}, f32[3,2,2,64,128]{4,3,2,1,0:T(8,128)S(1)}, f32[2,2,2,64,128]{4,3,2,1,0:T(8,128)S(1)}, s32[2,2,8]{2,1,0:T(2,128)S(1)}) custom-call(f32[3,2,2,64,128]{4,3,2,1,0:T(8,128)} %bitcast.16, f32[2,2,2,64,128]{4,3,2,1,0:T(8,128)} %bitcast.17, s32[2,2,8]{2,1,0:T(2,128)} %bitcast.18), custom_call_target="tpu_custom_call" | custom-call | bytes 1048576 | tf_op jit(solution)/shard_map/pallas_call | solution.py:486
  1.1 0.5 %collective-permute-start = (f32[64,8,128]{2,1,0:T(8,128)S(1)}, f32[64,8,128]{2,1,0:T(8,128)S(1)}, u32[]{:S(2)}, u32[]{:S(2)}) collective-permute-start(f32[64,8,128]{2,1,0:T(8,128)S(1)} %get-tuple-element.20), channel_id=1, source_target_pairs={{0,4},{1,5},{2,6},{3,7},{4,8},{5,9},{6,10},{7,11},{8,12},{9,13},{1... | collective-permute-start | bytes 786440 | tf_op jit(solution)/shard_map/ppermute | solution.py:438
  1.6 0.3 %shard_map.38 = (f32[28,8,128]{2,1,0:T(8,128)S(1)}, f32[28,8,128]{2,1,0:T(8,128)S(1)}, f32[28,8,128]{2,1,0:T(8,128)S(1)}, f32[28,8,128]{2,1,0:T(8,128)S(1)}, f32...) custom-call(f32[3,2,2,64,128]{4,3,2,1,0:T(8,128)S(1)} %get-tuple-element.16.state_ref, ...), custom_call_target="tpu_custom_call" | custom-call | bytes 1048576 | tf_op jit(solution)/shard_map/pallas_call | solution.py:492
  2.0 3.8 %collective-permute-start.1 = (f32[28,8,128]{2,1,0:T(8,128)S(1)}, f32[28,8,128]{2,1,0:T(8,128)S(1)}, u32[]{:S(2)}, u32[]{:S(2)}) collective-permute-start(f32[28,8,128]{2,1,0:T(8,128)S(1)} %get-tuple-element.22), channel_id=1, source_target_pairs={{0,5},{1,4},{2,7},{3,6},{4,9},{5,8},{6,11},{7,10},{8,13},{9,12},{1... | collective-permute-start | bytes 344072 | tf_op jit(solution)/shard_map/ppermute | solution.py:438
  5.8 0.0 collective-permute-start.2
  5.8 2.6 %collective-permute-start.3 = (f32[28,8,128]{2,1,0:T(8,128)S(1)}, f32[28,8,128]{2,1,0:T(8,128)S(1)}, u32[]{:S(2)}, u32[]{:S(2)}) collective-permute-start(f32[28,8,128]{2,1,0:T(8,128)S(1)} %get-tuple-element.24), channel_id=1, source_target_pairs={{0,1},{1,0},{2,3},{3,2},{4,5},{5,4},{6,7},{7,6},{8,9},{9,8},{10,11... | collective-permute-start | bytes 344072 | tf_op jit(solution)/shard_map/ppermute | solution.py:438
  8.4 1.3 %collective-permute-start.4 = (f32[28,8,128]{2,1,0:T(8,128)S(1)}, f32[28,8,128]{2,1,0:T(8,128)S(1)}, u32[]{:S(2)}, u32[]{:S(2)}) collective-permute-start(f32[28,8,128]{2,1,0:T(8,128)S(1)} %get-tuple-element.25), channel_id=1, source_target_pairs={{0,4},{1,9},{2,10},{3,7},{4,0},{5,6},{6,5},{7,3},{8,12},{9,17},{10... | collective-permute-start | bytes 344072 | tf_op jit(solution)/shard_map/ppermute | solution.py:438
  9.7 0.5 %collective-permute-done.1.xa.refs_1_ = f32[28,8,128]{2,1,0:T(8,128)S(1)} collective-permute-done((f32[28,8,128]{2,1,0:T(8,128)S(1)}, f32[28,8,128]{2,1,0:T(8,128)S(1)}, u32[]{:S(2)}, u32[]{:S(2)}) %collective-permute-start.1) | collective-permute-done | bytes 114720 | tf_op jit(solution)/shard_map/ppermute | solution.py:438
  10.2 0.0 collective-permute-start.6
  10.2 0.0 collective-permute-done.2.xb.refs_2_
  10.3 0.0 collective-permute-done.main.refs_0_
  10.3 1.2 %collective-permute-done.3.ka.refs_4_ = f32[28,8,128]{2,1,0:T(8,128)S(1)} collective-permute-done((f32[28,8,128]{2,1,0:T(8,128)S(1)}, f32[28,8,128]{2,1,0:T(8,128)S(1)}, u32[]{:S(2)}, u32[]{:S(2)}) %collective-permute-start.3) | collective-permute-done | bytes 114720 | tf_op jit(solution)/shard_map/ppermute | solution.py:438
  11.5 0.0 collective-permute-done.4.kb.refs_5_
  11.5 2.0 %collective-permute-start.5 = (f32[3,2,64,128]{3,2,1,0:T(8,128)S(1)}, f32[3,2,64,128]{3,2,1,0:T(8,128)S(1)}, u32[]{:S(2)}, u32[]{:S(2)}) collective-permute-start(f32[3,2,64,128]{3,2,1,0:T(8,128)S(1)} %shard_map.40), channel_id=1, source_target_pairs={{0,4},{1,5},{2,6},{3,7},{4,8},{5,9},{6,10},{7,11},{8,12},{9,13},{1... | collective-permute-start | bytes 589832 | tf_op jit(solution)/shard_map/ppermute | solution.py:438
  13.5 0.0 collective-permute-done.6.refs_6_
  13.5 1.7 %shard_map.41.second = f32[3,2,64,128]{3,2,1,0:T(8,128)S(1)} custom-call(f32[3,8,128]{2,1,0:T(8,128)S(1)} %get-tuple-element.19.plan, f32[64,8,128]{2,1,0:T(8,128)S(1)} %collective-permute-done.main.refs_0_, f32[28,8,128]{2,1,0:T(8,128)S(1)} %collective-permute-done.1.xa.refs_1_, f32[28,8,128]{2,1,0:T(8,128)S(1)} %collective-permute-done.2.xb.refs_2_, ...), custom_call_target="tpu_custom_call" | custom-call | flops 15728640 | bytes 1048576 | tf_op jit(solution)/shard_map/pallas_call | solution.py:525
  15.3 0.1 collective-permute-start.7
  15.4 1.7 %shard_map.42.third = f32[3,2,64,128]{3,2,1,0:T(8,128)S(1)} custom-call(f32[3,8,128]{2,1,0:T(8,128)S(1)} %get-tuple-element.19.plan, f32[64,8,128]{2,1,0:T(8,128)S(1)} %collective-permute-done.main.refs_0_, f32[28,8,128]{2,1,0:T(8,128)S(1)} %collective-permute-done.1.xa.refs_1_, f32[28,8,128]{2,1,0:T(8,128)S(1)} %collective-permute-done.2.xb.refs_2_, ...), custom_call_target="tpu_custom_call" | custom-call | flops 15728640 | bytes 1048576 | tf_op jit(solution)/shard_map/pallas_call | solution.py:527
  17.1 0.8 %collective-permute-done.5.far = f32[3,2,64,128]{3,2,1,0:T(8,128)S(1)} collective-permute-done((f32[3,2,64,128]{3,2,1,0:T(8,128)S(1)}, f32[3,2,64,128]{3,2,1,0:T(8,128)S(1)}, u32[]{:S(2)}, u32[]{:S(2)}) %collective-permute-start.5) | collective-permute-done | bytes 196640 | tf_op jit(solution)/shard_map/ppermute | solution.py:438
  17.9 0.0 collective-permute-done.7.near
  17.9 0.8 %shard_map.43 = f32[3,2,2,64,128]{4,3,2,1,0:T(8,128)} custom-call(f32[3,8,128]{2,1,0:T(8,128)S(1)} %get-tuple-element.19.plan, f32[3,2,64,128]{3,2,1,0:T(8,128)S(1)} %collective-permute-done.5.far, f32[3,2,64,128]{3,2,1,0:T(8,128)S(1)} %shard_map.41.second, f32[3,2,64,128]{3,2,1,0:T(8,128)S(1)} %collective-permute-done.7.near, ...), custom_call_target="tpu_custom_call" | custom-call | bytes 1048576 | tf_op jit(solution)/shard_map/pallas_call | solution.py:530
  (2 shorter events, 0.0 us)
Async XLA Ops:
  1.1 9.1 %collective-permute-start = (f32[64,8,128]{2,1,0:T(8,128)S(1)}, f32[64,8,128]{2,1,0:T(8,128)S(1)}, u32[]{:S(2)}, u32[]{:S(2)}) collective-permute-start(f32[64,8,128]{2,1,0:T(8,128)S(1)} %get-tuple-element.20), channel_id=1, source_target_pairs={{0,4},{1,5},{2,6},{3,7},{4,8},{5,9},{6,10},{7,11},{8,12},{9,13},{1... | collective-permute-start | bytes 786440 | tf_op jit(solution)/shard_map/ppermute | solution.py:438
  2.0 8.3 %collective-permute-start.1 = (f32[28,8,128]{2,1,0:T(8,128)S(1)}, f32[28,8,128]{2,1,0:T(8,128)S(1)}, u32[]{:S(2)}, u32[]{:S(2)}) collective-permute-start(f32[28,8,128]{2,1,0:T(8,128)S(1)} %get-tuple-element.22), channel_id=1, source_target_pairs={{0,5},{1,4},{2,7},{3,6},{4,9},{5,8},{6,11},{7,10},{8,13},{9,12},{1... | collective-permute-start | bytes 344072 | tf_op jit(solution)/shard_map/ppermute | solution.py:438
  5.8 4.5 %collective-permute-start.2 = (f32[28,8,128]{2,1,0:T(8,128)S(1)}, f32[28,8,128]{2,1,0:T(8,128)S(1)}, u32[]{:S(2)}, u32[]{:S(2)}) collective-permute-start(f32[28,8,128]{2,1,0:T(8,128)S(1)} %get-tuple-element.23), channel_id=1, source_target_pairs={{0,4},{1,6},{2,5},{3,7},{4,0},{5,10},{6,9},{7,3},{8,12},{9,14},{10... | collective-permute-start | bytes 344072 | tf_op jit(solution)/shard_map/ppermute | solution.py:438
  5.8 5.7 %collective-permute-start.3 = (f32[28,8,128]{2,1,0:T(8,128)S(1)}, f32[28,8,128]{2,1,0:T(8,128)S(1)}, u32[]{:S(2)}, u32[]{:S(2)}) collective-permute-start(f32[28,8,128]{2,1,0:T(8,128)S(1)} %get-tuple-element.24), channel_id=1, source_target_pairs={{0,1},{1,0},{2,3},{3,2},{4,5},{5,4},{6,7},{7,6},{8,9},{9,8},{10,11... | collective-permute-start | bytes 344072 | tf_op jit(solution)/shard_map/ppermute | solution.py:438
  8.4 3.1 %collective-permute-start.4 = (f32[28,8,128]{2,1,0:T(8,128)S(1)}, f32[28,8,128]{2,1,0:T(8,128)S(1)}, u32[]{:S(2)}, u32[]{:S(2)}) collective-permute-start(f32[28,8,128]{2,1,0:T(8,128)S(1)} %get-tuple-element.25), channel_id=1, source_target_pairs={{0,4},{1,9},{2,10},{3,7},{4,0},{5,6},{6,5},{7,3},{8,12},{9,17},{10... | collective-permute-start | bytes 344072 | tf_op jit(solution)/shard_map/ppermute | solution.py:438
  10.2 3.3 %collective-permute-start.6 = (f32[28,8,128]{2,1,0:T(8,128)S(1)}, f32[28,8,128]{2,1,0:T(8,128)S(1)}, u32[]{:S(2)}, u32[]{:S(2)}) collective-permute-start(f32[28,8,128]{2,1,0:T(8,128)S(1)} %get-tuple-element.25), channel_id=1, source_target_pairs={{0,4},{1,2},{2,1},{3,7},{4,0},{5,13},{6,14},{7,3},{8,12},{9,10},{1... | collective-permute-start | bytes 344072 | tf_op jit(solution)/shard_map/ppermute | solution.py:438
  11.5 6.4 %collective-permute-start.5 = (f32[3,2,64,128]{3,2,1,0:T(8,128)S(1)}, f32[3,2,64,128]{3,2,1,0:T(8,128)S(1)}, u32[]{:S(2)}, u32[]{:S(2)}) collective-permute-start(f32[3,2,64,128]{3,2,1,0:T(8,128)S(1)} %shard_map.40), channel_id=1, source_target_pairs={{0,4},{1,5},{2,6},{3,7},{4,8},{5,9},{6,10},{7,11},{8,12},{9,13},{1... | collective-permute-start | bytes 589832 | tf_op jit(solution)/shard_map/ppermute | solution.py:438
  15.3 2.7 %collective-permute-start.7 = (f32[3,2,64,128]{3,2,1,0:T(8,128)S(1)}, f32[3,2,64,128]{3,2,1,0:T(8,128)S(1)}, u32[]{:S(2)}, u32[]{:S(2)}) collective-permute-start(f32[3,2,64,128]{3,2,1,0:T(8,128)S(1)} %shard_map.41.second), channel_id=1, source_target_pairs={{0,4},{1,5},{2,6},{3,7},{4,0},{5,1},{6,2},{7,3},{8,12},{9,13},{10,... | collective-permute-start | bytes 589832 | tf_op jit(solution)/shard_map/ppermute | solution.py:438
